TPU v7x, 32 devices: a whole 2x2x4 slice. The times are simulated.
32 devices in a mesh: row: 4 (over y, core), col: 8 (over z, x).
Axes of the slice: x: 2, y: 2, z: 4, core: 2. Of those that a mesh axis runs over, the one named last changes fastest.
Arguments:
- inputs: bfloat16 [512, 8192], P(None, 'row'), may hold values from -6 to 6
- out_grad: bfloat16 [512, 8192], P(None, 'row'), may hold values from -6 to 6
- gate_weight: bfloat16 [8192, 28672], P('row', 'col'), may hold values from -0.125 to 0.125
- up_weight: bfloat16 [8192, 28672], P('row', 'col'), may hold values from -0.125 to 0.125
- down_weight: bfloat16 [28672, 8192], P('col', 'row'), may hold values from -0.0625 to 0.0625
- gate_mask: int32 [64, 224], P('row', 'col'), may hold values from 0 to 1, as said below
- up_mask: int32 [64, 224], P('row', 'col'), may hold values from 0 to 1, as said below
- down_mask: int32 [224, 64], P('col', 'row'), may hold values from 0 to 1, as said below
Outputs:
- input_grad: bfloat16 [512, 8192], P('col', 'row')
- gate_grad: bfloat16 [8192, 28672], P('row', 'col')
- up_grad: bfloat16 [8192, 28672], P('row', 'col')
- down_grad: bfloat16 [28672, 8192], P('col', 'row')
Inputs may be any that keep to these rules, and one draw needn't show every extreme that they name: `gate_mask`: 1 marks a kept 128 x 128 block of the gate projection; the share kept varies over row and column blocks. `up_mask`: 1 marks a kept 128 x 128 block of the up projection; the share kept varies over row and column blocks. `down_mask`: 1 marks a kept 128 x 128 block of the down projection; the share kept varies over row and column blocks.
All inputs are finite; a program needn't handle non-finite values.
Results may differ from a plain program's by a relative error of at most 0.0049.
Values may be sent and summed in bfloat16 or wider, within the bound.
No kernel may reach another device: no remote copies, remote signals or barrier semaphores. Data moves between devices by JAX's collectives and lax.ppermute only.
A program may use at most 256 MiB of HBM per device.

v0:
```python
import jax
import jax.numpy as jnp
from jax import lax
from jax.sharding import PartitionSpec as P


def spread(values, keep_mask):
    row_blocks, col_blocks = keep_mask.shape
    row_size = values.shape[0] // row_blocks
    col_size = values.shape[1] // col_blocks
    shaped = values.reshape(row_blocks, row_size, col_blocks, col_size)
    return (shaped * keep_mask.astype(values.dtype)[:, None, :, None]).reshape(values.shape)


def contract(former, latter, former_dim, latter_dim):
    return lax.dot_general(
        former,
        latter,
        (((former_dim,), (latter_dim,)), ((), ())),
        preferred_element_type=jnp.float32,
    )


def local_grads(gate_sum, up_sum, back_sum):
    sigmoid_gate = jax.nn.sigmoid(gate_sum)
    hidden = (gate_sum * sigmoid_gate * up_sum).astype(jnp.bfloat16)
    slope = sigmoid_gate * (1.0 + gate_sum * (1.0 - sigmoid_gate))
    gate_delta = (back_sum * up_sum * slope).astype(jnp.bfloat16)
    up_delta = (back_sum * gate_sum * sigmoid_gate).astype(jnp.bfloat16)
    return (hidden, gate_delta, up_delta)


def shards(inputs, out_grad, gate_weight, up_weight, down_weight, gate_mask, up_mask, down_mask):
    gate_full = spread(gate_weight, gate_mask)
    up_full = spread(up_weight, up_mask)
    down_full = spread(down_weight, down_mask)
    gate_cols = gate_full
    up_cols = up_full
    summed = lax.psum_scatter(
        jnp.stack(
            [
                contract(gate_cols, inputs, 0, 1),
                contract(up_cols, inputs, 0, 1),
                contract(down_full, out_grad, 1, 1),
            ],
            axis=1,
        ),
        "row",
        scatter_dimension=0,
        tiled=True,
    )
    hidden, gate_delta, up_delta = local_grads(summed[:, 0], summed[:, 1], summed[:, 2])
    piece_hidden = lax.all_gather(hidden, "row", axis=0, tiled=True)
    piece_gate = lax.all_gather(gate_delta, "row", axis=0, tiled=True)
    piece_up = lax.all_gather(up_delta, "row", axis=0, tiled=True)
    gate_cols = gate_full
    up_cols = up_full
    grad_gate = contract(inputs, piece_gate, 0, 1)
    grad_up = contract(inputs, piece_up, 0, 1)
    grad_down = contract(piece_hidden, out_grad, 1, 0)
    partial_value = contract(piece_gate, gate_cols, 0, 1) + contract(piece_up, up_cols, 0, 1)
    grad_gate, grad_up, grad_down, partial_value = (grad_gate, grad_up, grad_down, partial_value)
    input_grad = lax.psum_scatter(partial_value, "col", scatter_dimension=0, tiled=True).astype(
        jnp.bfloat16
    )
    gate_grad = spread(grad_gate, gate_mask).astype(jnp.bfloat16)
    up_grad = spread(grad_up, up_mask).astype(jnp.bfloat16)
    down_grad = spread(grad_down, down_mask).astype(jnp.bfloat16)
    return (input_grad, gate_grad, up_grad, down_grad)


def solution(mesh):
    placed = (
        P(None, "row"),
        P(None, "row"),
        P("row", "col"),
        P("row", "col"),
        P("col", "row"),
        P("row", "col"),
        P("row", "col"),
        P("col", "row"),
    )
    return jax.shard_map(
        shards,
        mesh=mesh,
        in_specs=placed,
        out_specs=(P("col", "row"), P("row", "col"), P("row", "col"), P("col", "row")),
        check_vma=False,
    )
```

profile of v0, /device:TPU:14, one launch (start us, length us, event | category | flops | bytes accessed | tf_op | source)
XLA Modules:
  0.0 540.8 jit_solution(74538472080179573)
XLA Ops:
  7.2 1.5 fusion.10
  8.7 0.1 copy.20
  8.8 20.2 %copy.21 = bf16[2048,3584]{0,1:T(8,128)(2,1)} copy(bf16[2048,3584]{1,0:T(8,128)(2,1)} %param.11) | data formatting | bytes 29360128 | tf_op args[3]
  29.0 0.1 copy.18
  29.1 20.4 %copy.19 = bf16[2048,3584]{0,1:T(8,128)(2,1)} copy(bf16[2048,3584]{1,0:T(8,128)(2,1)} %param.10) | data formatting | bytes 29360128 | tf_op args[2]
  49.5 0.1 copy.22
  49.6 7.4 %mul.93 = bf16[16,128,28,128]{1,0,3,2:T(8,128)(2,1)} broadcast(bf16[16,28]{0,1:T(8,128)(2,1)S(1)} %copy.20), dimensions={0,2} | broadcast | bytes 14680960 | tf_op jit(solution)/shard_map/mul | solution.py:12
  57.1 15.2 %convolution_bitcast_fusion = f32[3584,1,512]{2,0,1:T(8,128)} fusion(bf16[512,2048]{1,0:T(8,128)(2,1)S(1)} %copy-done, bf16[2048,3584]{0,1:T(8,128)(2,1)} %copy.21, bf16[448,8,16,128]{3,2,1,0:T(8,128)(2,1)} %bitcast.91), kind=kOutput, calls=%fused_computation.12 | convolution fusion | flops 7523532800 | bytes 38797312 | tf_op jit(solution)/shard_map/dot_general | solution.py:16
  72.3 7.2 %mul.90 = bf16[16,128,28,128]{1,0,3,2:T(8,128)(2,1)} broadcast(bf16[16,28]{0,1:T(8,128)(2,1)S(1)} %copy.18), dimensions={0,2} | broadcast | bytes 14680960 | tf_op jit(solution)/shard_map/mul | solution.py:12
  79.4 15.8 %convolution_bitcast_fusion.1 = f32[3584,1,512]{2,0,1:T(8,128)} fusion(bf16[512,2048]{1,0:T(8,128)(2,1)S(1)} %copy-done, bf16[2048,3584]{0,1:T(8,128)(2,1)} %copy.19, bf16[448,8,16,128]{3,2,1,0:T(8,128)(2,1)} %bitcast.93), kind=kOutput, calls=%fused_computation.13 | convolution fusion | flops 7523532800 | bytes 38797312 | tf_op jit(solution)/shard_map/dot_general | solution.py:16
  95.3 7.4 %mul.96 = bf16[28,128,16,128]{3,2,1,0:T(8,128)(2,1)} broadcast(bf16[28,16]{1,0:T(8,128)(2,1)S(1)} %copy.22), dimensions={0,2} | broadcast | bytes 14680960 | tf_op jit(solution)/shard_map/mul | solution.py:12
  102.7 15.8 %fusion.5 = f32[3584,1,512]{2,0,1:T(8,128)} fusion(bf16[512,2048]{1,0:T(8,128)(2,1)} %param.9, bf16[3584,2048]{1,0:T(8,128)(2,1)} %param.12, bf16[448,8,16,128]{3,2,1,0:T(8,128)(2,1)} %bitcast.95), kind=kOutput, calls=%fused_computation.14 | convolution fusion | flops 7523532800 | bytes 38797312 | tf_op jit(solution)/shard_map/dot_general | solution.py:16
  118.5 17.2 %pad_maximum_fusion = f32[3584,3,512]{2,0,1:T(8,128)} fusion(f32[3584,1,512]{2,0,1:T(8,128)} %fusion.5, f32[3584,1,512]{2,0,1:T(8,128)} %convolution_bitcast_fusion, f32[3584,1,512]{2,0,1:T(8,128)} %convolution_bitcast_fusion.1), kind=kLoop, calls=%fused_computation.6 | loop fusion | flops 11010048 | bytes 44040192 | tf_op jit(solution)/shard_map/stack | solution.py:40
  135.7 0.2 all-gather.4.cloned.1.call-start
  135.9 160.0 %reduce-scatter.3.cloned.1.call-done = f32[896,3,512]{2,0,1:T(8,128)} async-done(((f32[3584,3,512]{2,0,1:T(8,128)}), f32[896,3,512]{2,0,1:T(8,128)}) %reduce-scatter.3.cloned.1.call-update) | async-done | bytes 5505040 | tf_op jit(solution)/shard_map/reduce_scatter | solution.py:39
  295.9 5.3 multiply_convert_fusion
  301.3 0.7 all-gather.6.cloned.1.call-update
  302.0 0.5 all-gather.8.cloned.1.call-update
  302.6 30.3 %all-gather.4.cloned.1.call-done = bf16[3584,512]{1,0:T(8,128)(2,1)} async-done(((bf16[896,512]{1,0:T(8,128)(2,1)}), bf16[3584,512]{1,0:T(8,128)(2,1)}) %all-gather.4.cloned.1.call-update) | async-done | bytes 3670032 | tf_op jit(solution)/shard_map/all_gather | solution.py:54
  332.9 16.2 %fusion.6 = f32[512,2048]{1,0:T(8,128)} fusion(bf16[3584,512]{1,0:T(8,128)(2,1)} %all-gather.4.cloned.1.call-done, bf16[2048,3584]{0,1:T(8,128)(2,1)} %copy.19, bf16[448,8,16,128]{3,2,1,0:T(8,128)(2,1)} %bitcast.94), kind=kOutput, calls=%fused_computation.15 | convolution fusion | flops 7523532800 | bytes 37224448 | tf_op jit(solution)/shard_map/dot_general | solution.py:16
  349.1 17.0 %all-gather.6.cloned.1.call-done = bf16[3584,512]{1,0:T(8,128)(2,1)} async-done(((bf16[896,512]{1,0:T(8,128)(2,1)}), bf16[3584,512]{1,0:T(8,128)(2,1)}) %all-gather.6.cloned.1.call-update) | async-done | bytes 3670032 | tf_op jit(solution)/shard_map/all_gather | solution.py:55
  366.1 18.3 %fusion.8 = f32[512,2048]{1,0:T(8,128)} fusion(f32[512,2048]{1,0:T(8,128)} %fusion.6, bf16[3584,512]{1,0:T(8,128)(2,1)} %all-gather.6.cloned.1.call-done, bf16[2048,3584]{0,1:T(8,128)(2,1)} %copy.21, bf16[448,8,16,128]{3,2,1,0:T(8,128)(2,1)} %bitcast.92), kind=kOutput, calls=%fused_computation.17 | convolution fusion | flops 7524581376 | bytes 41418752 | tf_op jit(solution)/shard_map/dot_general | solution.py:16
  384.5 0.1 copy.23
  384.7 11.8 %mul.105 = f32[16,128,28,128]{1,0,3,2:T(8,128)} broadcast(f32[16,28]{0,1:T(8,128)S(1)} %copy.23), dimensions={0,2} | broadcast | bytes 29361920 | tf_op jit(solution)/shard_map/mul | solution.py:12
  396.5 24.7 %fusion.2 = bf16[2048,3584]{0,1:T(8,128)(2,1)} fusion(f32[448,8,16,128]{3,2,1,0:T(8,128)} %bitcast.88, bf16[3584,512]{1,0:T(8,128)(2,1)} %all-gather.4.cloned.1.call-done, bf16[512,2048]{1,0:T(8,128)(2,1)S(1)} %copy-done), kind=kOutput, calls=%fused_computation.5 | convolution fusion | flops 7530872832 | bytes 49807360 | tf_op jit(solution)/shard_map/dot_general | solution.py:16
  421.2 18.8 %copy.26 = bf16[2048,3584]{1,0:T(8,128)(2,1)} copy(bf16[2048,3584]{0,1:T(8,128)(2,1)} %fusion.2) | data formatting | bytes 29360128
  440.0 12.0 %mul.108 = f32[16,128,28,128]{1,0,3,2:T(8,128)} broadcast(f32[16,28]{0,1:T(8,128)S(1)} %copy.24), dimensions={0,2} | broadcast | bytes 29361920 | tf_op jit(solution)/shard_map/mul | solution.py:12
  452.0 24.6 %fusion.1 = bf16[2048,3584]{0,1:T(8,128)(2,1)} fusion(f32[448,8,16,128]{3,2,1,0:T(8,128)} %bitcast.89, bf16[3584,512]{1,0:T(8,128)(2,1)} %all-gather.6.cloned.1.call-done, bf16[512,2048]{1,0:T(8,128)(2,1)S(1)} %copy-done), kind=kOutput, calls=%fused_computation.3 | convolution fusion | flops 7530872832 | bytes 49807360 | tf_op jit(solution)/shard_map/dot_general | solution.py:16
  476.6 18.7 %copy.27 = bf16[2048,3584]{1,0:T(8,128)(2,1)} copy(bf16[2048,3584]{0,1:T(8,128)(2,1)} %fusion.1) | data formatting | bytes 29360128
  495.3 11.6 %mul.113 = f32[28,128,16,128]{3,2,1,0:T(8,128)} broadcast(f32[28,16]{1,0:T(8,128)S(1)} %copy.25), dimensions={0,2} | broadcast | bytes 29361920 | tf_op jit(solution)/shard_map/mul | solution.py:12
  506.9 25.1 %fusion = bf16[3584,2048]{1,0:T(8,128)(2,1)} fusion(f32[448,8,16,128]{3,2,1,0:T(8,128)} %bitcast.90, bf16[3584,512]{1,0:T(8,128)(2,1)} %all-gather.8.cloned.1.call-done, bf16[512,2048]{1,0:T(8,128)(2,1)} %param.9), kind=kOutput, calls=%fused_computation.1 | convolution fusion | flops 7530872832 | bytes 49807360 | tf_op jit(solution)/shard_map/dot_general | solution.py:16
  532.0 1.8 convert_element_type.44
  (21 shorter events, 0.4 us)
Async XLA Ops:
  7.2 49.9 %copy-start = (bf16[512,2048]{1,0:T(8,128)(2,1)S(1)}, bf16[512,2048]{1,0:T(8,128)(2,1)}, u32[]{:S(2)}) copy-start(bf16[512,2048]{1,0:T(8,128)(2,1)} %param.8) | copy-start | bytes 6291460
  7.2 288.7 %reduce-scatter.3.cloned.1.call-start = ((), (), s32[]{:S(2)}) async-start(), calls=%async_computation.2 | async-start | bytes 27525120 | tf_op jit(solution)/shard_map/reduce_scatter | solution.py:39
  8.8 20.2 %copy-start.2 = (s32[16,28]{1,0:T(8,128)S(1)}, s32[16,28]{1,0:T(8,128)}, u32[]{:S(2)}) copy-start(s32[16,28]{1,0:T(8,128)} %param.13) | copy-start | bytes 5380
  29.1 20.4 %copy-start.3 = (s32[28,16]{0,1:T(8,128)S(1)}, s32[28,16]{0,1:T(8,128)}, u32[]{:S(2)}) copy-start(s32[28,16]{0,1:T(8,128)} %param.15) | copy-start | bytes 5380
  135.7 197.2 %all-gather.4.cloned.1.call-start = ((), (), s32[]{:S(2)}) async-start(), calls=%async_computation.3 | async-start | bytes 4587520 | tf_op jit(solution)/shard_map/all_gather | solution.py:54
  301.2 64.9 %all-gather.6.cloned.1.call-start = ((), (), s32[]{:S(2)}) async-start(), calls=%async_computation.4 | async-start | bytes 4587520 | tf_op jit(solution)/shard_map/all_gather | solution.py:55
  302.0 193.3 %all-gather.8.cloned.1.call-start = ((), (), s32[]{:S(2)}) async-start(), calls=%async_computation.6 | async-start | bytes 4587520 | tf_op jit(solution)/shard_map/all_gather | solution.py:53
  302.6 229.4 %reduce-scatter.5.cloned.1.call-start = ((), (), s32[]{:S(2)}) async-start(), calls=%async_computation.5 | async-start | bytes 4718592 | tf_op jit(solution)/shard_map/reduce_scatter | solution.py:63
  349.1 35.4 %copy-start.1 = (f32[16,28]{1,0:T(8,128)S(1)}, f32[16,28]{1,0:T(8,128)}, u32[]{:S(2)}) copy-start(f32[16,28]{1,0:T(8,128)} %get-tuple-element.17) | copy-start | bytes 5380
Sparse Core Ops, SparseCore 0:
  135.8 160.0 reduce-scatter.2
  301.4 31.5 all-gather.3
  334.6 31.4 all-gather.5
  367.6 31.4 all-gather.7
  403.1 89.1 reduce-scatter.4
where the time goes:
time: 552 us; the launch traced here: 541 us
  waiting for transfers between devices  209 us (38%)
  matrix products  156 us (28%)
  local copies, waits for them, and re-layouts  136 us (25%)
  other arithmetic  25.7 us (5%)
  between operations  14.3 us (3%)
    reduce_scatter x1, waiting for transfers between devices, shards(): lax.psum_scatter(jnp.stack([contract(gate_cols, inputs, 0, 1), contract(u...  160 us
    dot_general x8, matrix products, contract(): lax.dot_general(former, latter, (((former_dim,), (latter_dim,)), ((), ())...  156 us
    unnamed x12, local copies, waits for them, and re-layouts  78.1 us
    mul x6, local copies, waits for them, and re-layouts, spread(): shaped * keep_mask.astype(values.dtype)[:, None, :, None]  57.4 us
    all_gather x1, waiting for transfers between devices, shards(): piece_gate = lax.all_gather(gate_delta, 'row', axis=0, tiled=True)  30.3 us
    another operation x1, other arithmetic, shards(): jnp.stack([contract(gate_cols, inputs, 0, 1), contract(up_cols, inputs, 0...  17.2 us
    all_gather x1, waiting for transfers between devices, shards(): piece_up = lax.all_gather(up_delta, 'row', axis=0, tiled=True)  17 us
  transfers between devices with their start and end apart: 5, of which 3 were waited for; matrix products, arithmetic and copies ran while one was open for 34% of the time, Pallas kernels for 0%

commit v1 on v0

v1 whole, which is shorter than its diff:
```python
import jax
import jax.numpy as jnp
from jax import lax
from jax.experimental import pallas as pl
from jax.experimental.pallas import tpu as pltpu
from jax.sharding import PartitionSpec as P

BLOCK = 128
TILE = 256
VMEM_LIMIT = 50 * 1024 * 1024
F32 = jnp.float32
BF16 = jnp.bfloat16
ANY = pl.BlockSpec(memory_space=pl.ANY)


def cost():
    return pl.CostEstimate(flops=10**8, bytes_accessed=10**5, transcendentals=0)


def params():
    return pltpu.CompilerParams(vmem_limit_bytes=VMEM_LIMIT)


def put_masked(out_ref, w_ref, mask_ref, row_base, col_base):
    rows, cols = w_ref.shape
    for i in range(rows // BLOCK):
        for j in range(cols // BLOCK):
            r, c = slice(i * BLOCK, (i + 1) * BLOCK), slice(j * BLOCK, (j + 1) * BLOCK)
            keep = mask_ref[row_base + i, col_base + j] != 0
            block = w_ref[r, c]
            out_ref[r, c] = jnp.where(keep, block, jnp.zeros_like(block))


def cols_spec(rows, first):
    return pl.BlockSpec((rows, TILE), lambda n, *_: (0, n + first))


def rows_spec(cols, first):
    return pl.BlockSpec((TILE, cols), lambda n, *_: (n + first, 0))


def whole_spec(shape, once=False):
    mode = {"pipeline_mode": pl.Buffered(1)} if once else {}
    return pl.BlockSpec(shape, lambda n, *_: (0,) * len(shape), **mode)


def forward(core, x, g, weights, masks, first, tiles, n_pair, deps):
    tokens, d = x.shape
    own = tokens // 2
    per_col = own // n_pair

    def kernel(core_ref, gm, um, dm, x_ref, g_ref, gw_ref, uw_ref, dw_ref, *rest):
        keep_ref, give_ref, gs, us, ds = rest[len(deps) :]
        c0 = (pl.program_id(0) + first) * (TILE // BLOCK)
        low = core_ref[0] == 0

        def put(k, sums):
            top, bottom = sums[:own], sums[own:]
            keep_ref[0, k] = jnp.where(low, top, bottom).reshape(n_pair, per_col, TILE)
            give_ref[0, k] = jnp.where(low, bottom, top).astype(give_ref.dtype).reshape(n_pair, per_col, TILE)

        put_masked(gs, gw_ref, gm, 0, c0)
        put_masked(us, uw_ref, um, 0, c0)
        put_masked(ds, dw_ref, dm, c0, 0)
        put(0, jnp.dot(x_ref[...], gs[...], preferred_element_type=F32))
        put(1, jnp.dot(x_ref[...], us[...], preferred_element_type=F32))
        put(2, lax.dot_general(g_ref[...], ds[...], (((1,), (1,)), ((), ())), preferred_element_type=F32))

    shape = (tiles, 3, n_pair, per_col, TILE)
    out_spec = pl.BlockSpec((1, *shape[1:]), lambda n, *_: (n, 0, 0, 0, 0))
    width = tiles * TILE
    return pl.pallas_call(
        kernel,
        grid_spec=pltpu.PrefetchScalarGridSpec(
            num_scalar_prefetch=4,
            grid=(tiles,),
            in_specs=[
                whole_spec((tokens, d), True),
                whole_spec((tokens, d), True),
                cols_spec(d, first),
                cols_spec(d, first),
                rows_spec(d, first),
            ]
            + [ANY] * len(deps),
            out_specs=[out_spec, out_spec],
            scratch_shapes=[pltpu.VMEM((d, TILE), BF16), pltpu.VMEM((d, TILE), BF16), pltpu.VMEM((TILE, d), BF16)],
        ),
        out_shape=[jax.ShapeDtypeStruct(shape, F32), jax.ShapeDtypeStruct(shape, BF16)],
        compiler_params=params(),
        cost_estimate=cost(),
        name="forward",
    )(core, *masks, x, g, *weights, *deps)


def source_spec(array, begin):
    size = array.shape[0]
    return pl.BlockSpec(
        (1, *array.shape[1:]), lambda n, *_: (jnp.clip(n - begin, 0, size - 1), 0, 0, 0, 0)
    )


def backward(core, sources, x, g, weights, masks, first, acc, grads, x_index, wanted, n_col, deps):
    tokens, d = x.shape
    ff = weights[0].shape[1]
    n_pair = n_col // 2
    per_col = tokens // n_col
    sizes = [own.shape[0] for own, _ in sources]
    begins = [sum(sizes[:k]) for k in range(len(sizes))]
    tiles = sum(sizes)
    with_input, with_weight = "input" in wanted, "weight" in wanted
    last = x_index is not None
    over_tokens = (((0,), (0,)), ((), ()))
    over_hidden = (((1,), (1,)), ((), ()))

    def kernel(core_ref, xi, gm, um, dm, *refs):
        n = pl.program_id(0)
        refs = list(refs)
        value_refs = [refs.pop(0) for _ in range(2 * len(sources))]
        if with_weight:
            x_ref, g_ref = refs.pop(0), refs.pop(0)
        if with_input:
            gw_ref, uw_ref = refs.pop(0), refs.pop(0)
        acc_ref = refs.pop(0) if with_input and acc is not None else None
        del refs[: len(deps) + (3 if with_weight and grads is not None else 0)]
        if with_input:
            if last:
                give_ref, keep_ref = refs.pop(0), refs.pop(0)
                total = refs.pop()
            else:
                total = refs.pop(0)
        if with_weight:
            gg_ref, ug_ref, dg_ref = refs.pop(0), refs.pop(0), refs.pop(0)
        hidden_s, deltas_s = refs.pop(0), refs.pop(0)
        ws = refs.pop(0) if with_input else None
        c0 = (n + first) * (TILE // BLOCK)
        for s in range(len(sources)):

            @pl.when((n >= begins[s]) & (n < begins[s] + sizes[s]))
            def _():
                for who in range(2):
                    ref = value_refs[2 * s + who]
                    half = core_ref[0] if who == 0 else 1 - core_ref[0]
                    hidden_s[half] = ref[0, 0]
                    deltas_s[half, :, :, :TILE] = ref[0, 1]
                    deltas_s[half, :, :, TILE:] = ref[0, 2]

        deltas = deltas_s[...].reshape(tokens, 2 * TILE)
        if with_input:
            put_masked(ws.at[:, :TILE], gw_ref, gm, 0, c0)
            put_masked(ws.at[:, TILE:], uw_ref, um, 0, c0)

            @pl.when(n == 0)
            def _():
                total[...] = jnp.zeros_like(total) if acc is None else acc_ref[...]

            total[...] += lax.dot_general(deltas, ws[...], over_hidden, preferred_element_type=F32)
            if last:

                @pl.when(n == tiles - 1)
                def _():
                    for p in range(n_pair):
                        give_at = pl.multiple_of((2 * p + 1 - xi[0]) * per_col, 16)
                        keep_at = pl.multiple_of((2 * p + xi[0]) * per_col, 16)
                        give_ref[p] = total[pl.ds(give_at, per_col), :].astype(BF16)
                        keep_ref[p] = total[pl.ds(keep_at, per_col), :]

        if with_weight:
            hidden = hidden_s[...].reshape(tokens, TILE)
            gate = lax.dot_general(x_ref[...], deltas[:, :TILE], over_tokens, preferred_element_type=F32)
            put_masked(gg_ref, gate.astype(BF16), gm, 0, c0)
            up = lax.dot_general(x_ref[...], deltas[:, TILE:], over_tokens, preferred_element_type=F32)
            put_masked(ug_ref, up.astype(BF16), um, 0, c0)
            down = jnp.dot(hidden.T, g_ref[...], preferred_element_type=F32)
            put_masked(dg_ref, down.astype(BF16), dm, c0, 0)

    in_specs, operands, aliases = [], [], {}
    out_specs, out_shape = [], []
    scratch = [pltpu.VMEM((2, n_pair, per_col, TILE), BF16), pltpu.VMEM((2, n_pair, per_col, 2 * TILE), BF16)]
    for pair, begin in zip(sources, begins):
        in_specs += [source_spec(v, begin) for v in pair]
        operands += pair
    if with_weight:
        in_specs += [whole_spec((tokens, d), True)] * 2
        operands += [x, g]
    if with_input:
        in_specs += [cols_spec(d, first), cols_spec(d, first)]
        operands += weights[:2]
        scratch.append(pltpu.VMEM((d, 2 * TILE), BF16))
        if acc is not None:
            in_specs.append(whole_spec((tokens, d), True))
            operands.append(acc)
        if last:
            shape = (n_pair, per_col, d)
            out_specs += [whole_spec(shape), whole_spec(shape)]
            out_shape += [jax.ShapeDtypeStruct(shape, BF16), jax.ShapeDtypeStruct(shape, F32)]
            scratch.append(pltpu.VMEM((tokens, d), F32))
        else:
            out_specs.append(whole_spec((tokens, d)))
            out_shape.append(jax.ShapeDtypeStruct((tokens, d), F32))
    if with_weight:
        if grads is not None:
            for k, e in enumerate(grads):
                aliases[5 + len(operands)] = len(out_shape) + k
                in_specs.append(ANY)
                operands.append(e)
        out_specs += [cols_spec(d, first), cols_spec(d, first), rows_spec(d, first)]
        out_shape += [jax.ShapeDtypeStruct(s, BF16) for s in ((d, ff), (d, ff), (ff, d))]
    in_specs += [ANY] * len(deps)
    operands += deps
    width = tiles * TILE
    outs = pl.pallas_call(
        kernel,
        grid_spec=pltpu.PrefetchScalarGridSpec(
            num_scalar_prefetch=5,
            grid=(tiles,),
            in_specs=in_specs,
            out_specs=out_specs,
            scratch_shapes=scratch,
        ),
        out_shape=out_shape,
        input_output_aliases=aliases,
        compiler_params=params(),
        cost_estimate=cost(),
        name="backward_" + "_".join(wanted),
    )(core, core if x_index is None else x_index, *masks, *operands)
    n_in = (2 if last else 1) if with_input else 0
    return outs[:n_in], outs[n_in:]


def local_grads(sums):
    gate_sum, up_sum, back_sum = sums[:, 0], sums[:, 1], sums[:, 2]
    sigmoid_gate = jax.nn.sigmoid(gate_sum)
    silu = gate_sum * sigmoid_gate
    hidden = silu * up_sum
    slope = sigmoid_gate * (1.0 + gate_sum * (1.0 - sigmoid_gate))
    return jnp.stack([hidden, back_sum * up_sum * slope, back_sum * silu], axis=1).astype(BF16)


def after(token, *arrays):
    return lax.optimization_barrier((*arrays, token))[: len(arrays)]


def plan(tiles):
    if tiles < 14:
        sizes = [1, 2, tiles - 3]
        pieces = [(0, 0, 1), (1, 0, 2), (2, 0, tiles - 3)]
        steps = [("F", 0), ("F", 1), ("S", 0), ("F", 2), ("S", 1), ("L", 0), ("S", 2), ("L", 1), ("B", [0, 1]), ("L", 2), ("I", [2]), ("W", [2])]
        return sizes, pieces, steps
    sizes = [1, 1, 2, 3, 3, tiles - 10]
    pieces = [(0, 0, 1), (1, 0, 1), (2, 0, 2), (3, 0, 3), (4, 0, 3), (5, 0, tiles - 12), (5, tiles - 12, 2)]
    steps = [("F", 0), ("F", 1), ("S", 0), ("F", 2), ("S", 1), ("F", 3), ("S", 2), ("F", 4), ("S", 3), ("F", 5)]
    steps += [("L", 0), ("L", 1), ("S", 4), ("L", 2), ("B", [0, 1, 2]), ("L", 3), ("S", 5), ("B", [3]), ("S", 6)]
    steps += [("L", 4), ("B", [4]), ("L", 5), ("B", [5]), ("L", 6), ("I", [6]), ("W", [6])]
    return sizes, pieces, steps


def build(n_row, n_col):
    n_y = n_row // 2
    n_pair = n_col // 2

    def swap_core(v):
        return lax.ppermute(v, "row", [(i, i ^ 1) for i in range(n_row)])

    def from_y(v):
        return [
            lax.ppermute(v, "row", [(i, (i + 2 * s) % n_row) for i in range(n_row)]) for s in range(1, n_y)
        ]

    def shards(inputs, out_grad, gate_w, up_w, down_w, gate_mask, up_mask, down_mask):
        ff = gate_w.shape[1]
        core_arg = (lax.axis_index("row") % 2).reshape(1).astype(jnp.int32)
        col = lax.axis_index("col")
        x_pos, z_pos = col % 2, col // 2
        x_arg = x_pos.reshape(1).astype(jnp.int32)
        masks = (gate_mask, up_mask, down_mask)
        weights = [gate_w, up_w, down_w]
        sizes, pieces, steps = plan(ff // TILE)
        firsts = [sum(sizes[:c]) for c in range(len(sizes))]
        kept, crossed = {}, {}
        mine, arrived, values = {}, {}, {}
        acc, grads = None, None
        token = None

        for kind, what in steps:
            deps = [] if token is None else [token]
            if kind == "F":
                kept[what], give = forward(
                    core_arg, inputs, out_grad, weights, masks, firsts[what], sizes[what], n_pair, deps
                )
                crossed[what] = swap_core(give)
                token = kept[what]
            elif kind == "S":
                c, at, size = pieces[what]
                keep, cross = after(token, kept[c], crossed[c])
                mine[what] = keep[at : at + size] + cross[at : at + size].astype(F32)
                sent = mine[what].astype(BF16)
                arrived[what] = from_y(sent)
                token = sent
            elif kind == "L":
                total, *others = after(token, mine[what], *arrived[what])
                for other in others:
                    total = total + other.astype(F32)
                own = local_grads(total)
                values[what] = (own, swap_core(own))
                token = own
            else:
                wanted = {"B": ("input", "weight"), "I": ("input",), "W": ("weight",)}[kind]
                c, at, _ = pieces[what[0]]
                part, new = backward(
                    core_arg,
                    [values[i] for i in what],
                    inputs,
                    out_grad,
                    weights,
                    masks,
                    firsts[c] + at,
                    acc,
                    grads,
                    x_arg if kind == "I" else None,
                    wanted,
                    n_col,
                    deps,
                )
                if kind == "I":
                    give, keep = part
                else:
                    grads = new
                    acc = part[0] if part else None
                token = new[0] if new else part[0]

        from_x = lax.ppermute(give, "col", [(j, j ^ 1) for j in range(n_col)])
        keep, from_x = after(token, keep, from_x)
        summed = keep + from_x.astype(F32)
        total = lax.dynamic_index_in_dim(summed, z_pos, 0, keepdims=False)
        for s in range(1, n_pair):
            out = lax.dynamic_index_in_dim(summed, z_pos ^ s, 0, keepdims=False).astype(BF16)
            total = total + lax.ppermute(out, "col", [(j, j ^ (2 * s)) for j in range(n_col)]).astype(F32)
        return (total.astype(BF16), *grads)

    return shards


def solution(mesh):
    placed = (
        P(None, "row"),
        P(None, "row"),
        P("row", "col"),
        P("row", "col"),
        P("col", "row"),
        P("row", "col"),
        P("row", "col"),
        P("col", "row"),
    )
    return jax.shard_map(
        build(mesh.shape["row"], mesh.shape["col"]),
        mesh=mesh,
        in_specs=placed,
        out_specs=(P("col", "row"), P("row", "col"), P("row", "col"), P("col", "row")),
        check_vma=False,
    )
```

time: 552 us -> 249 us (0.45); the launches traced: 541 us -> 245 us
  matrix products: 156 us -> 0 us
  waiting for transfers between devices: 209 us -> 58.4 us
  Pallas kernels: 0 us -> 150 us
  local copies, waits for them, and re-layouts: 136 us -> 6.23 us
  between operations: 14.3 us -> 1.32 us
  starting transfers between devices: 0.37 us -> 12.5 us
  other arithmetic: 25.7 us -> 16.8 us
    reduce_scatter x2 -> x0, waiting for transfers between devices: 160 us -> none  [the longest x1 160 us: shards(): lax.psum_scatter(jnp.stack([contract(gate_cols, inputs, 0, 1), contract(u...]
    dot_general x8 -> x0, matrix products: 156 us -> none  [contract(): lax.dot_general(former, latter, (((former_dim,), (latter_dim,)), ((), ())...]
    pallas_call x0 -> x12, Pallas kernels: none -> 150 us  [the longest x6 92.6 us: backward(): pl.pallas_call(kernel, grid_spec=pltpu.PrefetchScalarGridSpec(num_scalar_...]
    unnamed x12 -> x27, local copies, waits for them, and re-layouts: 78.1 us -> 6.12 us
    ppermute x0 -> x24, waiting for transfers between devices: none -> 58.4 us  [the longest x3 22.2 us: shards(): lax.ppermute(out, 'col', [(j, j ^ 2 * s) for j in range(n_col)]).astype(F32)]
    mul x6 -> x0, local copies, waits for them, and re-layouts: 57.4 us -> none  [spread(): shaped * keep_mask.astype(values.dtype)[:, None, :, None]]
    all_gather x3 -> x0, waiting for transfers between devices: 47.3 us -> none  [the longest x1 30.3 us: shards(): piece_gate = lax.all_gather(gate_delta, 'row', axis=0, tiled=True)]
    another operation x1 -> x14, other arithmetic: 17.2 us -> 2.91 us  [shards(): jnp.stack([contract(gate_cols, inputs, 0, 1), contract(up_cols, inputs, 0...]
  transfers between devices with their start and end apart: 5 -> 24, of which waited for: 3 -> 14; matrix products, arithmetic and copies ran while one was open for 34% -> 5% of each run, Pallas kernels for 0% -> 50%
where the time goes in v1:
time: 249 us; the launch traced here: 245 us
  Pallas kernels  150 us (60%)
  waiting for transfers between devices  58.4 us (23%)
  other arithmetic  16.8 us (7%)
  starting transfers between devices  12.5 us (5%)
  local copies, waits for them, and re-layouts  6.23 us (3%)
    pallas_call x6, Pallas kernels, backward(): pl.pallas_call(kernel, grid_spec=pltpu.PrefetchScalarGridSpec(num_scalar_...  92.6 us
    pallas_call x6, Pallas kernels, forward(): pl.pallas_call(kernel, grid_spec=pltpu.PrefetchScalarGridSpec(num_scalar_...  57.5 us
    ppermute x3, waiting for transfers between devices, shards(): lax.ppermute(out, 'col', [(j, j ^ 2 * s) for j in range(n_col)]).astype(F32)  22.2 us
    ppermute x1, waiting for transfers between devices, shards(): from_x = lax.ppermute(give, 'col', [(j, j ^ 1) for j in range(n_col)])  15.8 us
    ppermute x7, waiting for transfers between devices, from_y(): lax.ppermute(v, 'row', [(i, (i + 2 * s) % n_row) for i in range(n_row)])  10.2 us
    ppermute x13, waiting for transfers between devices, swap_core(): return lax.ppermute(v, 'row', [(i, i ^ 1) for i in range(n_row)])  10.2 us
    add x7, other arithmetic, shards(): total = total + other.astype(F32)  6.2 us
    unnamed x27, local copies, waits for them, and re-layouts  6.12 us
  transfers between devices with their start and end apart: 24, of which 14 were waited for; matrix products, arithmetic and copies ran while one was open for 5% of the time, Pallas kernels for 50%

profile of v1, /device:TPU:14, one launch (start us, length us, event | category | flops | bytes accessed | tf_op | source)
XLA Modules:
  0.0 245.3 jit_solution(13495651104751015515)
XLA Ops:
  1.4 1.6 copy-done
  4.4 5.6 %forward.6 = (f32[1,3,4,64,256]{4,3,2,1,0:T(8,128)S(1)}, bf16[1,3,4,64,256]{4,3,2,1,0:T(8,128)(2,1)S(1)}) custom-call(s32[1]{0:T(128)} %bitcast.core_ref.xi, s32[16,28]{1,0:T(8,128)S(1)} %copy-done.3, s32[16,28]{1,0:T(8,128)S(1)} %copy-done.5, s32[28,16]{1,0:T(8,128)S(1)} %copy.34.dm, bf16[512,2048]{1,0:T(8,128)(2,1)S(1)} %copy-done, ...), custom_call_target="tpu_custom_call" | custom-call | flops 100000000 | bytes 100000 | tf_op jit(solution)/shard_map/forward/pallas_call | solution.py:72
  10.1 5.6 %forward.7 = (f32[1,3,4,64,256]{4,3,2,1,0:T(8,128)S(1)}, bf16[1,3,4,64,256]{4,3,2,1,0:T(8,128)(2,1)S(1)}) custom-call(s32[1]{0:T(128)} %bitcast.core_ref.xi, s32[16,28]{1,0:T(8,128)S(1)} %copy-done.3, s32[16,28]{1,0:T(8,128)S(1)} %copy-done.5, s32[28,16]{1,0:T(8,128)S(1)} %copy.34.dm, bf16[512,2048]{1,0:T(8,128)(2,1)S(1)} %copy-done, ...), custom_call_target="tpu_custom_call" | custom-call | flops 100000000 | bytes 100000 | tf_op jit(solution)/shard_map/forward/pallas_call | solution.py:72
  16.4 9.3 %forward.8 = (f32[2,3,4,64,256]{4,3,2,1,0:T(8,128)S(1)}, bf16[2,3,4,64,256]{4,3,2,1,0:T(8,128)(2,1)S(1)}) custom-call(s32[1]{0:T(128)} %bitcast.core_ref.xi, s32[16,28]{1,0:T(8,128)S(1)} %copy-done.3, s32[16,28]{1,0:T(8,128)S(1)} %copy-done.5, s32[28,16]{1,0:T(8,128)S(1)} %copy.34.dm, bf16[512,2048]{1,0:T(8,128)(2,1)} %refs_2_.9, bf16[512,2048]{1,0:T(8,128)(2,1)} %refs_3_.9, ...), custom_call_target="tpu_custom_call" | custom-call | flops 100000000 | bytes 100000 | tf_op jit(solution)/shard_map/forward/pallas_call | solution.py:72
  25.9 1.5 copy-done.1
  27.4 11.5 %forward.9 = (f32[3,3,4,64,256]{4,3,2,1,0:T(8,128)}, bf16[3,3,4,64,256]{4,3,2,1,0:T(8,128)(2,1)S(1)}) custom-call(s32[1]{0:T(128)} %bitcast.core_ref.xi, s32[16,28]{1,0:T(8,128)S(1)} %copy-done.3, s32[16,28]{1,0:T(8,128)S(1)} %copy-done.5, s32[28,16]{1,0:T(8,128)S(1)} %copy.34.dm, bf16[512,2048]{1,0:T(8,128)(2,1)S(1)} %copy-done.1, ...), custom_call_target="tpu_custom_call" | custom-call | flops 100000000 | bytes 100000 | tf_op jit(solution)/shard_map/forward/pallas_call | solution.py:72
  39.9 1.5 collective-permute-start.8
  42.8 1.4 fusion.17
  44.8 11.5 %forward.10 = (f32[3,3,4,64,256]{4,3,2,1,0:T(8,128)}, bf16[3,3,4,64,256]{4,3,2,1,0:T(8,128)(2,1)S(1)}) custom-call(s32[1]{0:T(128)} %bitcast.core_ref.xi, s32[16,28]{1,0:T(8,128)S(1)} %copy-done.3, s32[16,28]{1,0:T(8,128)S(1)} %copy-done.5, s32[28,16]{1,0:T(8,128)S(1)} %copy.34.dm, bf16[512,2048]{1,0:T(8,128)(2,1)S(1)} %copy-done.1, ...), custom_call_target="tpu_custom_call" | custom-call | flops 100000000 | bytes 100000 | tf_op jit(solution)/shard_map/forward/pallas_call | solution.py:72
  56.8 1.6 collective-permute-start.5
  58.4 13.9 %forward.11 = (f32[4,3,4,64,256]{4,3,2,1,0:T(8,128)}, bf16[4,3,4,64,256]{4,3,2,1,0:T(8,128)(2,1)S(1)}) custom-call(s32[1]{0:T(128)} %bitcast.core_ref.xi, s32[16,28]{1,0:T(8,128)S(1)} %copy-done.3, s32[16,28]{1,0:T(8,128)S(1)} %copy-done.5, s32[28,16]{1,0:T(8,128)S(1)} %copy.34.dm, bf16[512,2048]{1,0:T(8,128)(2,1)} %refs_2_.9, bf16[512,2048]{1,0:T(8,128)(2,1)} %refs_3_.9, ...), custom_call_target="tpu_custom_call" | custom-call | flops 100000000 | bytes 100000 | tf_op jit(solution)/shard_map/forward/pallas_call | solution.py:72
  79.6 1.8 collective-permute-done.9.refs_3_
  82.0 21.4 %backward_input_weight.4 = (f32[512,2048]{1,0:T(8,128)}, bf16[2048,3584]{1,0:T(8,128)(2,1)}, bf16[2048,3584]{1,0:T(8,128)(2,1)}, bf16[3584,2048]{1,0:T(8,128)(2,1)}) custom-call(s32[1]{0:T(128)} %bitcast.core_ref.xi, s32[1]{0:T(128)} %bitcast.core_ref.xi, s32[16,28]{1,0:T(8,128)S(1)} %copy-done.3, s32[16,28]{1,0:T(8,128)S(1)} %copy-done.5, ...), custom_call_target="tpu_custom_call" | custom-call | flops 100000000 | bytes 100000 | tf_op jit(solution)/shard_map/backward_input_weight/pallas_call | solution.py:211
  103.5 1.7 convert_add_fusion.1
  107.0 1.5 fusion.14
  108.7 18.9 %backward_input_weight.5 = (f32[512,2048]{1,0:T(8,128)}, bf16[2048,3584]{1,0:T(8,128)(2,1)}, bf16[2048,3584]{1,0:T(8,128)(2,1)}, bf16[3584,2048]{1,0:T(8,128)(2,1)}) custom-call(s32[1]{0:T(128)} %bitcast.core_ref.xi, s32[1]{0:T(128)} %bitcast.core_ref.xi, s32[16,28]{1,0:T(8,128)S(1)} %copy-done.3, ...), custom_call_target="tpu_custom_call", output_to_operand_aliasing={{1}: (12, {}), {2}: (13, {}), {3}: (14, {})} | custom-call | flops 100000000 | bytes 100000 | tf_op jit(solution)/shard_map/backward_input_weight/pallas_call | solution.py:211
  127.9 6.3 %collective-permute-done.16 = bf16[3,3,4,64,256]{4,3,2,1,0:T(8,128)(2,1)S(1)} collective-permute-done((bf16[3,3,4,64,256]{4,3,2,1,0:T(8,128)(2,1)S(1)}, bf16[3,3,4,64,256]{4,3,2,1,0:T(8,128)(2,1)S(1)}, u32[]{:S(2)}, u32[]{:S(2)}) %collective-permute-start.16) | collective-permute-done | bytes 1179680 | tf_op jit(solution)/shard_map/ppermute | solution.py:266
  136.0 2.3 collective-permute-done.17.refs_1_
  138.2 19.1 %backward_input_weight.6 = (f32[512,2048]{1,0:T(8,128)}, bf16[2048,3584]{1,0:T(8,128)(2,1)}, bf16[2048,3584]{1,0:T(8,128)(2,1)}, bf16[3584,2048]{1,0:T(8,128)(2,1)}) custom-call(s32[1]{0:T(128)} %bitcast.core_ref.xi, s32[1]{0:T(128)} %bitcast.core_ref.xi, s32[16,28]{1,0:T(8,128)S(1)} %copy-done.3, ...), custom_call_target="tpu_custom_call", output_to_operand_aliasing={{1}: (12, {}), {2}: (13, {}), {3}: (14, {})} | custom-call | flops 100000000 | bytes 100000 | tf_op jit(solution)/shard_map/backward_input_weight/pallas_call | solution.py:211
  158.7 1.6 collective-permute-done.18.refs_1_
  160.4 14.7 %backward_input_weight.7 = (f32[512,2048]{1,0:T(8,128)}, bf16[2048,3584]{1,0:T(8,128)(2,1)}, bf16[2048,3584]{1,0:T(8,128)(2,1)}, bf16[3584,2048]{1,0:T(8,128)(2,1)}) custom-call(s32[1]{0:T(128)} %bitcast.core_ref.xi, s32[1]{0:T(128)} %bitcast.core_ref.xi, s32[16,28]{1,0:T(8,128)S(1)} %copy-done.3, ...), custom_call_target="tpu_custom_call", output_to_operand_aliasing={{1}: (12, {}), {2}: (13, {}), {3}: (14, {})} | custom-call | flops 100000000 | bytes 100000 | tf_op jit(solution)/shard_map/backward_input_weight/pallas_call | solution.py:211
  175.1 3.0 %collective-permute-done.14 = bf16[2,3,4,64,256]{4,3,2,1,0:T(8,128)(2,1)S(1)} collective-permute-done((bf16[2,3,4,64,256]{4,3,2,1,0:T(8,128)(2,1)S(1)}, bf16[2,3,4,64,256]{4,3,2,1,0:T(8,128)(2,1)S(1)}, u32[]{:S(2)}, u32[]{:S(2)}) %collective-permute-start.14) | collective-permute-done | bytes 786464 | tf_op jit(solution)/shard_map/ppermute | solution.py:266
  178.8 2.3 collective-permute-done.19.refs_1_
  181.1 9.5 %backward_input.1 = (bf16[4,64,2048]{2,1,0:T(8,128)(2,1)S(1)}, f32[4,64,2048]{2,1,0:T(8,128)}) custom-call(s32[1]{0:T(128)} %bitcast.core_ref.xi, s32[1]{0:T(128)} %bitcast.1.xi, s32[16,28]{1,0:T(8,128)S(1)} %copy-done.4, s32[16,28]{1,0:T(8,128)S(1)} %copy-done.6, s32[28,16]{1,0:T(8,128)S(1)} %copy.34.dm, ...), custom_call_target="tpu_custom_call" | custom-call | flops 100000000 | bytes 100000 | tf_op jit(solution)/shard_map/backward_input/pallas_call | solution.py:211
  191.1 9.0 %backward_weight.1 = (bf16[2048,3584]{1,0:T(8,128)(2,1)}, bf16[2048,3584]{1,0:T(8,128)(2,1)}, bf16[3584,2048]{1,0:T(8,128)(2,1)}) custom-call(s32[1]{0:T(128)} %bitcast.core_ref.xi, s32[1]{0:T(128)} %bitcast.core_ref.xi, s32[16,28]{1,0:T(8,128)S(1)} %copy-done.4, ...), custom_call_target="tpu_custom_call", output_to_operand_aliasing={{0}: (9, {}), {1}: (10, {}), {2}: (11, {})} | custom-call | flops 100000000 | bytes 100000 | tf_op jit(solution)/shard_map/backward_weight/pallas_call | solution.py:211
  200.1 15.8 %collective-permute-done.20 = bf16[4,64,2048]{2,1,0:T(8,128)(2,1)} collective-permute-done((bf16[4,64,2048]{2,1,0:T(8,128)(2,1)S(1)}, bf16[4,64,2048]{2,1,0:T(8,128)(2,1)}, u32[]{:S(2)}, u32[]{:S(2)}) %collective-permute-start.20) | collective-permute-done | bytes 1048608 | tf_op jit(solution)/shard_map/ppermute | solution.py:331
  215.9 1.5 convert_add_fusion.4
  218.0 2.6 %collective-permute-start.22 = (bf16[64,2048]{1,0:T(8,128)(2,1)S(1)}, bf16[64,2048]{1,0:T(8,128)(2,1)S(1)}, u32[]{:S(2)}, u32[]{:S(2)}) collective-permute-start(bf16[64,2048]{1,0:T(8,128)(2,1)S(1)} %get-tuple-element.152), channel_id=1, source_target_pairs={{0,4},{1,5},{2,6},{3,7},{4,0},{5,1},{6,2},{7,3},{8,12},{9,13},{10,... | collective-permute-start | bytes 786440 | tf_op jit(solution)/shard_map/ppermute | solution.py:337
  221.1 6.6 %collective-permute-done.21 = bf16[64,2048]{1,0:T(8,128)(2,1)S(1)} collective-permute-done((bf16[64,2048]{1,0:T(8,128)(2,1)S(1)}, bf16[64,2048]{1,0:T(8,128)(2,1)S(1)}, u32[]{:S(2)}, u32[]{:S(2)}) %collective-permute-start.21) | collective-permute-done | bytes 262176 | tf_op jit(solution)/shard_map/ppermute | solution.py:337
  227.7 11.0 %collective-permute-done.22 = bf16[64,2048]{1,0:T(8,128)(2,1)S(1)} collective-permute-done((bf16[64,2048]{1,0:T(8,128)(2,1)S(1)}, bf16[64,2048]{1,0:T(8,128)(2,1)S(1)}, u32[]{:S(2)}, u32[]{:S(2)}) %collective-permute-start.22) | collective-permute-done | bytes 262176 | tf_op jit(solution)/shard_map/ppermute | solution.py:337
  238.6 4.7 %collective-permute-done.23 = bf16[64,2048]{1,0:T(8,128)(2,1)} collective-permute-done((bf16[64,2048]{1,0:T(8,128)(2,1)S(1)}, bf16[64,2048]{1,0:T(8,128)(2,1)}, u32[]{:S(2)}, u32[]{:S(2)}) %collective-permute-start.23) | collective-permute-done | bytes 262176 | tf_op jit(solution)/shard_map/ppermute | solution.py:337
  243.3 1.8 fusion.4
  (86 shorter events, 22.0 us)
Async XLA Ops:
  10.0 6.3 %collective-permute-start.1 = (bf16[1,3,4,64,256]{4,3,2,1,0:T(8,128)(2,1)S(1)}, bf16[1,3,4,64,256]{4,3,2,1,0:T(8,128)(2,1)S(1)}, u32[]{:S(2)}, u32[]{:S(2)}) collective-permute-start(bf16[1,3,4,64,256]{4,3,2,1,0:T(8,128)(2,1)S(1)} %get-tuple-element.70), channel_id=1, source_target_pairs={{0,8},{8,0},{16,24},{24,16},{1,9},{9,1},{17,25},{25,17},{2,10},{10... | collective-permute-start | bytes 1179656 | tf_op jit(solution)/shard_map/ppermute | solution.py:262
  15.8 10.0 %collective-permute-start = (bf16[1,3,4,64,256]{4,3,2,1,0:T(8,128)(2,1)S(1)}, bf16[1,3,4,64,256]{4,3,2,1,0:T(8,128)(2,1)S(1)}, u32[]{:S(2)}, u32[]{:S(2)}) collective-permute-start(bf16[1,3,4,64,256]{4,3,2,1,0:T(8,128)(2,1)S(1)} %get-tuple-element.69), channel_id=1, source_target_pairs={{0,8},{8,0},{16,24},{24,16},{1,9},{9,1},{17,25},{25,17},{2,10},{10... | collective-permute-start | bytes 1179656 | tf_op jit(solution)/shard_map/ppermute | solution.py:262
  38.9 17.4 %collective-permute-start.2 = (bf16[3,3,4,64,256]{4,3,2,1,0:T(8,128)(2,1)S(1)}, bf16[3,3,4,64,256]{4,3,2,1,0:T(8,128)(2,1)S(1)}, u32[]{:S(2)}, u32[]{:S(2)}) collective-permute-start(bf16[3,3,4,64,256]{4,3,2,1,0:T(8,128)(2,1)S(1)} %get-tuple-element.77), channel_id=1, source_target_pairs={{0,8},{8,0},{16,24},{24,16},{1,9},{9,1},{17,25},{25,17},{2,10},{10... | collective-permute-start | bytes 3538952 | tf_op jit(solution)/shard_map/ppermute | solution.py:262
  38.9 4.0 %collective-permute-start.3 = (bf16[2,3,4,64,256]{4,3,2,1,0:T(8,128)(2,1)S(1)}, bf16[2,3,4,64,256]{4,3,2,1,0:T(8,128)(2,1)S(1)}, u32[]{:S(2)}, u32[]{:S(2)}) collective-permute-start(bf16[2,3,4,64,256]{4,3,2,1,0:T(8,128)(2,1)S(1)} %get-tuple-element.78), channel_id=1, source_target_pairs={{0,8},{8,0},{16,24},{24,16},{1,9},{9,1},{17,25},{25,17},{2,10},{10... | collective-permute-start | bytes 2359304 | tf_op jit(solution)/shard_map/ppermute | solution.py:262
  39.4 32.9 %collective-permute-start.6 = (bf16[1,3,4,64,256]{4,3,2,1,0:T(8,128)(2,1)S(1)}, bf16[1,3,4,64,256]{4,3,2,1,0:T(8,128)(2,1)}, u32[]{:S(2)}, u32[]{:S(2)}) collective-permute-start(bf16[1,3,4,64,256]{4,3,2,1,0:T(8,128)(2,1)S(1)} %get-tuple-element.142.rest_0_), channel_id=1, source_target_pairs={{0,16},{8,24},{16,0},{24,8},{1,17},{9,25},{17,1},{25,9},{2,18},{10... | collective-permute-start | bytes 1179656 | tf_op jit(solution)/shard_map/ppermute | solution.py:266
  39.9 33.7 %collective-permute-start.8 = (bf16[1,3,4,64,256]{4,3,2,1,0:T(8,128)(2,1)S(1)}, bf16[1,3,4,64,256]{4,3,2,1,0:T(8,128)(2,1)}, u32[]{:S(2)}, u32[]{:S(2)}) collective-permute-start(bf16[1,3,4,64,256]{4,3,2,1,0:T(8,128)(2,1)S(1)} %get-tuple-element.140.rest_0_), channel_id=1, source_target_pairs={{0,16},{8,24},{16,0},{24,8},{1,17},{9,25},{17,1},{25,9},{2,18},{10... | collective-permute-start | bytes 1179656 | tf_op jit(solution)/shard_map/ppermute | solution.py:266
  44.3 32.4 %collective-permute-start.10 = (bf16[2,3,4,64,256]{4,3,2,1,0:T(8,128)(2,1)S(1)}, bf16[2,3,4,64,256]{4,3,2,1,0:T(8,128)(2,1)}, u32[]{:S(2)}, u32[]{:S(2)}) collective-permute-start(bf16[2,3,4,64,256]{4,3,2,1,0:T(8,128)(2,1)S(1)} %get-tuple-element.138.rest_0_), channel_id=1, source_target_pairs={{0,16},{8,24},{16,0},{24,8},{1,17},{9,25},{17,1},{25,9},{2,18},{10... | collective-permute-start | bytes 2359304 | tf_op jit(solution)/shard_map/ppermute | solution.py:266
  44.8 11.5 %copy-start.11 = (f32[3,3,4,64,256]{4,3,2,1,0:T(8,128)S(1)}, f32[3,3,4,64,256]{4,3,2,1,0:T(8,128)}, u32[]{:S(2)}) copy-start(f32[3,3,4,64,256]{4,3,2,1,0:T(8,128)} %get-tuple-element.82) | copy-start | bytes 7077892
  56.3 18.8 %collective-permute-start.11 = (bf16[3,3,4,64,256]{4,3,2,1,0:T(8,128)(2,1)S(1)}, bf16[3,3,4,64,256]{4,3,2,1,0:T(8,128)(2,1)S(1)}, u32[]{:S(2)}, u32[]{:S(2)}) collective-permute-start(bf16[3,3,4,64,256]{4,3,2,1,0:T(8,128)(2,1)S(1)} %get-tuple-element.90), channel_id=1, source_target_pairs={{0,8},{8,0},{16,24},{24,16},{1,9},{9,1},{17,25},{25,17},{2,10},{10... | collective-permute-start | bytes 3538952 | tf_op jit(solution)/shard_map/ppermute | solution.py:262
  56.8 46.7 %collective-permute-start.5 = (bf16[3,3,4,64,256]{4,3,2,1,0:T(8,128)(2,1)S(1)}, bf16[3,3,4,64,256]{4,3,2,1,0:T(8,128)(2,1)}, u32[]{:S(2)}, u32[]{:S(2)}) collective-permute-start(bf16[3,3,4,64,256]{4,3,2,1,0:T(8,128)(2,1)S(1)} %get-tuple-element.136.rest_0_), channel_id=1, source_target_pairs={{0,16},{8,24},{16,0},{24,8},{1,17},{9,25},{17,1},{25,9},{2,18},{10... | collective-permute-start | bytes 3538952 | tf_op jit(solution)/shard_map/ppermute | solution.py:266
  73.6 1.8 copy-start.10
  78.6 3.5 %collective-permute-start.12 = (bf16[2,3,4,64,256]{4,3,2,1,0:T(8,128)(2,1)S(1)}, bf16[2,3,4,64,256]{4,3,2,1,0:T(8,128)(2,1)S(1)}, u32[]{:S(2)}, u32[]{:S(2)}) collective-permute-start(bf16[2,3,4,64,256]{4,3,2,1,0:T(8,128)(2,1)S(1)} %pad_maximum_fusion.2.refs_4_.refs_10_), channel_id=1, source_target_pairs={{0,8},{8,0},{16,24},{24,16},{1,9},{9,1},{17,25},{25,17},{2,10},{10... | collective-permute-start | bytes 2359304 | tf_op jit(solution)/shard_map/ppermute | solution.py:262
  78.7 2.8 %collective-permute-start.9 = (bf16[1,3,4,64,256]{4,3,2,1,0:T(8,128)(2,1)S(1)}, bf16[1,3,4,64,256]{4,3,2,1,0:T(8,128)(2,1)S(1)}, u32[]{:S(2)}, u32[]{:S(2)}) collective-permute-start(bf16[1,3,4,64,256]{4,3,2,1,0:T(8,128)(2,1)S(1)} %pad_maximum_fusion.6.refs_2_), channel_id=1, source_target_pairs={{0,8},{8,0},{16,24},{24,16},{1,9},{9,1},{17,25},{25,17},{2,10},{10... | collective-permute-start | bytes 1179656 | tf_op jit(solution)/shard_map/ppermute | solution.py:262
  79.1 2.9 %collective-permute-start.7 = (bf16[1,3,4,64,256]{4,3,2,1,0:T(8,128)(2,1)S(1)}, bf16[1,3,4,64,256]{4,3,2,1,0:T(8,128)(2,1)S(1)}, u32[]{:S(2)}, u32[]{:S(2)}) collective-permute-start(bf16[1,3,4,64,256]{4,3,2,1,0:T(8,128)(2,1)S(1)} %pad_maximum_fusion.5.refs_0_), channel_id=1, source_target_pairs={{0,8},{8,0},{16,24},{24,16},{1,9},{9,1},{17,25},{25,17},{2,10},{10... | collective-permute-start | bytes 1179656 | tf_op jit(solution)/shard_map/ppermute | solution.py:262
  79.2 27.3 %collective-permute-start.4 = (bf16[4,3,4,64,256]{4,3,2,1,0:T(8,128)(2,1)S(1)}, bf16[4,3,4,64,256]{4,3,2,1,0:T(8,128)(2,1)S(1)}, u32[]{:S(2)}, u32[]{:S(2)}) collective-permute-start(bf16[4,3,4,64,256]{4,3,2,1,0:T(8,128)(2,1)S(1)} %get-tuple-element.85), channel_id=1, source_target_pairs={{0,8},{8,0},{16,24},{24,16},{1,9},{9,1},{17,25},{25,17},{2,10},{10... | collective-permute-start | bytes 4718600 | tf_op jit(solution)/shard_map/ppermute | solution.py:262
  105.1 1.9 copy-start.9
  105.8 2.9 %collective-permute-start.13 = (bf16[3,3,4,64,256]{4,3,2,1,0:T(8,128)(2,1)S(1)}, bf16[3,3,4,64,256]{4,3,2,1,0:T(8,128)(2,1)S(1)}, u32[]{:S(2)}, u32[]{:S(2)}) collective-permute-start(bf16[3,3,4,64,256]{4,3,2,1,0:T(8,128)(2,1)S(1)} %pad_maximum_fusion.refs_0_), channel_id=1, source_target_pairs={{0,8},{8,0},{16,24},{24,16},{1,9},{9,1},{17,25},{25,17},{2,10},{10... | collective-permute-start | bytes 3538952 | tf_op jit(solution)/shard_map/ppermute | solution.py:262
  106.0 28.3 %collective-permute-start.16 = (bf16[3,3,4,64,256]{4,3,2,1,0:T(8,128)(2,1)S(1)}, bf16[3,3,4,64,256]{4,3,2,1,0:T(8,128)(2,1)S(1)}, u32[]{:S(2)}, u32[]{:S(2)}) collective-permute-start(bf16[3,3,4,64,256]{4,3,2,1,0:T(8,128)(2,1)S(1)} %get-tuple-element.134), channel_id=1, source_target_pairs={{0,16},{8,24},{16,0},{24,8},{1,17},{9,25},{17,1},{25,9},{2,18},{10... | collective-permute-start | bytes 3538952 | tf_op jit(solution)/shard_map/ppermute | solution.py:266
  135.3 2.9 %collective-permute-start.17 = (bf16[3,3,4,64,256]{4,3,2,1,0:T(8,128)(2,1)S(1)}, bf16[3,3,4,64,256]{4,3,2,1,0:T(8,128)(2,1)S(1)}, u32[]{:S(2)}, u32[]{:S(2)}) collective-permute-start(bf16[3,3,4,64,256]{4,3,2,1,0:T(8,128)(2,1)S(1)} %pad_maximum_fusion.1.refs_0_.refs_10_), channel_id=1, source_target_pairs={{0,8},{8,0},{16,24},{24,16},{1,9},{9,1},{17,25},{25,17},{2,10},{10... | collective-permute-start | bytes 3538952 | tf_op jit(solution)/shard_map/ppermute | solution.py:262
  135.4 21.9 %collective-permute-start.15 = (bf16[2,3,4,64,256]{4,3,2,1,0:T(8,128)(2,1)S(1)}, bf16[2,3,4,64,256]{4,3,2,1,0:T(8,128)(2,1)S(1)}, u32[]{:S(2)}, u32[]{:S(2)}) collective-permute-start(bf16[2,3,4,64,256]{4,3,2,1,0:T(8,128)(2,1)S(1)} %get-tuple-element.132.refs_10_), channel_id=1, source_target_pairs={{0,16},{8,24},{16,0},{24,8},{1,17},{9,25},{17,1},{25,9},{2,18},{10... | collective-permute-start | bytes 2359304 | tf_op jit(solution)/shard_map/ppermute | solution.py:266
  138.2 19.1 %copy-start.8 = (f32[2,3,4,64,256]{4,3,2,1,0:T(8,128)S(1)}, f32[2,3,4,64,256]{4,3,2,1,0:T(8,128)}, u32[]{:S(2)}) copy-start(f32[2,3,4,64,256]{4,3,2,1,0:T(8,128)} %get-tuple-element.112) | copy-start | bytes 4718596
  157.6 2.8 %copy-start.2 = (bf16[512,2048]{1,0:T(8,128)(2,1)S(1)}, bf16[512,2048]{1,0:T(8,128)(2,1)}, u32[]{:S(2)}) copy-start(bf16[512,2048]{1,0:T(8,128)(2,1)} %refs_2_.9) | copy-start | bytes 6291460
  158.0 2.4 collective-permute-start.18
  158.2 19.8 %collective-permute-start.14 = (bf16[2,3,4,64,256]{4,3,2,1,0:T(8,128)(2,1)S(1)}, bf16[2,3,4,64,256]{4,3,2,1,0:T(8,128)(2,1)S(1)}, u32[]{:S(2)}, u32[]{:S(2)}) collective-permute-start(bf16[2,3,4,64,256]{4,3,2,1,0:T(8,128)(2,1)S(1)} %get-tuple-element.130), channel_id=1, source_target_pairs={{0,16},{8,24},{16,0},{24,8},{1,17},{9,25},{17,1},{25,9},{2,18},{10... | collective-permute-start | bytes 2359304 | tf_op jit(solution)/shard_map/ppermute | solution.py:266
  178.3 2.8 %copy-start.4 = (s32[16,28]{1,0:T(8,128)S(1)}, s32[16,28]{1,0:T(8,128)}, u32[]{:S(2)}) copy-start(s32[16,28]{1,0:T(8,128)} %gm.23) | copy-start | bytes 5380
  178.3 2.8 %copy-start.6 = (s32[16,28]{1,0:T(8,128)S(1)}, s32[16,28]{1,0:T(8,128)}, u32[]{:S(2)}) copy-start(s32[16,28]{1,0:T(8,128)} %um.23) | copy-start | bytes 5380
  178.7 2.4 collective-permute-start.19
  190.6 25.3 %collective-permute-start.20 = (bf16[4,64,2048]{2,1,0:T(8,128)(2,1)S(1)}, bf16[4,64,2048]{2,1,0:T(8,128)(2,1)}, u32[]{:S(2)}, u32[]{:S(2)}) collective-permute-start(bf16[4,64,2048]{2,1,0:T(8,128)(2,1)S(1)} %get-tuple-element.122.refs_7_), channel_id=1, source_target_pairs={{0,1},{1,0},{2,3},{3,2},{4,5},{5,4},{6,7},{7,6},{8,9},{9,8},{10,11... | collective-permute-start | bytes 3145736 | tf_op jit(solution)/shard_map/ppermute | solution.py:331
  191.1 24.8 %copy-start.12 = (f32[4,64,2048]{2,1,0:T(8,128)S(1)}, f32[4,64,2048]{2,1,0:T(8,128)}, u32[]{:S(2)}) copy-start(f32[4,64,2048]{2,1,0:T(8,128)} %get-tuple-element.126) | copy-start | bytes 6291460
  217.5 10.1 %collective-permute-start.21 = (bf16[64,2048]{1,0:T(8,128)(2,1)S(1)}, bf16[64,2048]{1,0:T(8,128)(2,1)S(1)}, u32[]{:S(2)}, u32[]{:S(2)}) collective-permute-start(bf16[64,2048]{1,0:T(8,128)(2,1)S(1)} %get-tuple-element.150), channel_id=1, source_target_pairs={{0,2},{1,3},{2,0},{3,1},{4,6},{5,7},{6,4},{7,5},{8,10},{9,11},{10,... | collective-permute-start | bytes 786440 | tf_op jit(solution)/shard_map/ppermute | solution.py:337
  218.0 20.6 %collective-permute-start.22 = (bf16[64,2048]{1,0:T(8,128)(2,1)S(1)}, bf16[64,2048]{1,0:T(8,128)(2,1)S(1)}, u32[]{:S(2)}, u32[]{:S(2)}) collective-permute-start(bf16[64,2048]{1,0:T(8,128)(2,1)S(1)} %get-tuple-element.152), channel_id=1, source_target_pairs={{0,4},{1,5},{2,6},{3,7},{4,0},{5,1},{6,2},{7,3},{8,12},{9,13},{10,... | collective-permute-start | bytes 786440 | tf_op jit(solution)/shard_map/ppermute | solution.py:337
  220.6 22.7 %collective-permute-start.23 = (bf16[64,2048]{1,0:T(8,128)(2,1)S(1)}, bf16[64,2048]{1,0:T(8,128)(2,1)}, u32[]{:S(2)}, u32[]{:S(2)}) collective-permute-start(bf16[64,2048]{1,0:T(8,128)(2,1)S(1)} %get-tuple-element.151), channel_id=1, source_target_pairs={{0,6},{1,7},{2,4},{3,5},{4,2},{5,3},{6,0},{7,1},{8,14},{9,15},{10,... | collective-permute-start | bytes 786440 | tf_op jit(solution)/shard_map/ppermute | solution.py:337
  (5 other events, 6.3 us)

commit v2 on v1

v2 whole, which is shorter than its diff:
```python
import jax
import jax.numpy as jnp
from jax import lax
from jax.experimental import pallas as pl
from jax.experimental.pallas import tpu as pltpu
from jax.sharding import PartitionSpec as P

BLOCK = 128
TILE = 256
VMEM_LIMIT = 40 * 1024 * 1024
F32 = jnp.float32
BF16 = jnp.bfloat16
ANY = pl.BlockSpec(memory_space=pl.ANY)
COSTS = {'F': 8400000, 'B': 16800000, 'I': 8400000, 'W': 8400000}


def cost(kind, tiles):
    return pl.CostEstimate(flops=COSTS[kind] * tiles, bytes_accessed=0, transcendentals=0)


def params():
    return pltpu.CompilerParams(vmem_limit_bytes=VMEM_LIMIT)


def put_masked(out_ref, w_ref, mask_ref, row_base, col_base):
    rows, cols = w_ref.shape
    for i in range(rows // BLOCK):
        for j in range(cols // BLOCK):
            r, c = slice(i * BLOCK, (i + 1) * BLOCK), slice(j * BLOCK, (j + 1) * BLOCK)
            keep = mask_ref[row_base + i, col_base + j] != 0
            block = w_ref[r, c]
            out_ref[r, c] = jnp.where(keep, block, jnp.zeros_like(block))


def cols_spec(rows, first):
    return pl.BlockSpec((rows, TILE), lambda n, *_: (0, n + first))


def rows_spec(cols, first):
    return pl.BlockSpec((TILE, cols), lambda n, *_: (n + first, 0))


def whole_spec(shape, once=False):
    mode = {"pipeline_mode": pl.Buffered(1)} if once else {}
    return pl.BlockSpec(shape, lambda n, *_: (0,) * len(shape), **mode)


def forward(core, x, g, weights, masks, first, tiles, n_pair, deps, arrange):
    tokens, d = x.shape
    own = tokens // 2
    per_col = own // n_pair

    def kernel(core_ref, gm, um, dm, x_ref, g_ref, gw_ref, uw_ref, dw_ref, *rest):
        keep_ref, *give_refs = rest[len(deps) :][:4]
        *arranged, gs, us, ds = rest[len(deps) + 4 :]
        c0 = (pl.program_id(0) + first) * (TILE // BLOCK)
        if arrange:

            @pl.when(pl.program_id(0) == 0)
            def _():
                for to_ref, from_ref in zip(arranged, (x_ref, g_ref)):
                    for who in range(2):
                        half = core_ref[0] if who == 0 else 1 - core_ref[0]
                        at = pl.multiple_of(half * own, own)
                        to_ref[who * own : (who + 1) * own, :] = from_ref[pl.ds(at, own), :]

            x_ref, g_ref = arranged

        def put(k, sums):
            keep_ref[0, k] = sums[:own].reshape(n_pair, per_col, TILE)
            give_refs[k][0] = sums[own:].astype(BF16).reshape(n_pair, per_col, TILE)

        put_masked(gs, gw_ref, gm, 0, c0)
        put_masked(us, uw_ref, um, 0, c0)
        put_masked(ds, dw_ref, dm, c0, 0)
        put(0, jnp.dot(x_ref[...], gs[...], preferred_element_type=F32))
        put(1, jnp.dot(x_ref[...], us[...], preferred_element_type=F32))
        put(2, lax.dot_general(g_ref[...], ds[...], (((1,), (1,)), ((), ())), preferred_element_type=F32))

    shape = (tiles, 3, n_pair, per_col, TILE)
    keep_spec = pl.BlockSpec((1, *shape[1:]), lambda n, *_: (n, 0, 0, 0, 0))
    give_spec = pl.BlockSpec((1, *shape[2:]), lambda n, *_: (n, 0, 0, 0))
    width = tiles * TILE
    return pl.pallas_call(
        kernel,
        grid_spec=pltpu.PrefetchScalarGridSpec(
            num_scalar_prefetch=4,
            grid=(tiles,),
            in_specs=[
                whole_spec((tokens, d), True),
                whole_spec((tokens, d), True),
                cols_spec(d, first),
                cols_spec(d, first),
                rows_spec(d, first),
            ]
            + [ANY] * len(deps),
            out_specs=[keep_spec] + [give_spec] * 3 + [whole_spec((tokens, d))] * (2 * arrange),
            scratch_shapes=[pltpu.VMEM((d, TILE), BF16), pltpu.VMEM((d, TILE), BF16), pltpu.VMEM((TILE, d), BF16)],
        ),
        out_shape=[jax.ShapeDtypeStruct(shape, F32)]
        + [jax.ShapeDtypeStruct((tiles, *shape[2:]), BF16)] * 3
        + [jax.ShapeDtypeStruct((tokens, d), BF16)] * (2 * arrange),
        compiler_params=params(),
        cost_estimate=cost("F", tiles),
        name=f"forward_t{tiles}",
    )(core, *masks, x, g, *weights, *deps)


def source_spec(array, begin):
    size = array.shape[0]
    return pl.BlockSpec(
        (1, *array.shape[1:]), lambda n, *_: (jnp.clip(n - begin, 0, size - 1), 0, 0, 0)
    )


def backward(sources, x, g, weights, masks, first, acc, grads, x_index, wanted, n_col, deps, n_part):
    tokens, d = x.shape
    ff = weights[0].shape[1]
    n_pair = n_col // 2
    per_col = tokens // n_col
    sizes = [own[0].shape[0] for own, _ in sources]
    begins = [sum(sizes[:k]) for k in range(len(sizes))]
    tiles = sum(sizes)
    with_input, with_weight = "input" in wanted, "weight" in wanted
    used = (0, 1, 2) if with_weight else (1, 2)
    last = x_index is not None
    part_rows = per_col // n_part
    over_tokens = (((0,), (0,)), ((), ()))
    over_hidden = (((1,), (1,)), ((), ()))

    def kernel(xi, gm, um, dm, *refs):
        n = pl.program_id(0)
        refs = list(refs)
        value_refs = [[{q: refs.pop(0) for q in used} for _ in range(2)] for _ in sources]
        if with_weight:
            x_ref, g_ref = refs.pop(0), refs.pop(0)
        if with_input:
            gw_ref, uw_ref = refs.pop(0), refs.pop(0)
        acc_ref = refs.pop(0) if with_input and acc is not None else None
        del refs[: len(deps) + (3 if with_weight and grads is not None else 0)]
        if with_input:
            if last:
                give_refs, keep_refs = ([refs.pop(0) for _ in range(n_part)] for _ in range(2))
                total = refs.pop()
            else:
                total = refs.pop(0)
        if with_weight:
            gg_ref, ug_ref, dg_ref = refs.pop(0), refs.pop(0), refs.pop(0)
        hidden_s, deltas_s = refs.pop(0), refs.pop(0)
        ws = refs.pop(0) if with_input else None
        c0 = (n + first) * (TILE // BLOCK)
        for s in range(len(sources)):

            @pl.when((n >= begins[s]) & (n < begins[s] + sizes[s]))
            def _():
                for who in range(2):
                    value = value_refs[s][who]
                    if with_weight:
                        hidden_s[who] = value[0][0]
                    deltas_s[who, :, :, :TILE] = value[1][0]
                    deltas_s[who, :, :, TILE:] = value[2][0]

        deltas = deltas_s[...].reshape(tokens, 2 * TILE)
        if with_input:
            put_masked(ws.at[:, :TILE], gw_ref, gm, 0, c0)
            put_masked(ws.at[:, TILE:], uw_ref, um, 0, c0)

            @pl.when(n == 0)
            def _():
                total[...] = jnp.zeros_like(total) if acc is None else acc_ref[...]

            total[...] += lax.dot_general(deltas, ws[...], over_hidden, preferred_element_type=F32)
            if last:

                @pl.when(n == tiles - 1)
                def _():
                    for p in range(n_pair):
                        for q in range(n_part):
                            give_at = pl.multiple_of((2 * p + 1 - xi[0]) * per_col + q * part_rows, 16)
                            keep_at = pl.multiple_of((2 * p + xi[0]) * per_col + q * part_rows, 16)
                            give_refs[q][p] = total[pl.ds(give_at, part_rows), :].astype(BF16)
                            keep_refs[q][p] = total[pl.ds(keep_at, part_rows), :]

        if with_weight:
            hidden = hidden_s[...].reshape(tokens, TILE)
            gate = lax.dot_general(x_ref[...], deltas[:, :TILE], over_tokens, preferred_element_type=F32)
            put_masked(gg_ref, gate.astype(BF16), gm, 0, c0)
            up = lax.dot_general(x_ref[...], deltas[:, TILE:], over_tokens, preferred_element_type=F32)
            put_masked(ug_ref, up.astype(BF16), um, 0, c0)
            down = jnp.dot(hidden.T, g_ref[...], preferred_element_type=F32)
            put_masked(dg_ref, down.astype(BF16), dm, c0, 0)

    in_specs, operands, aliases = [], [], {}
    out_specs, out_shape = [], []
    scratch = [pltpu.VMEM((2, n_pair, per_col, TILE), BF16), pltpu.VMEM((2, n_pair, per_col, 2 * TILE), BF16)]
    for pair, begin in zip(sources, begins):
        for value in pair:
            in_specs += [source_spec(value[q], begin) for q in used]
            operands += [value[q] for q in used]
    if with_weight:
        in_specs += [whole_spec((tokens, d), True)] * 2
        operands += [x, g]
    if with_input:
        in_specs += [cols_spec(d, first), cols_spec(d, first)]
        operands += weights[:2]
        scratch.append(pltpu.VMEM((d, 2 * TILE), BF16))
        if acc is not None:
            in_specs.append(whole_spec((tokens, d), True))
            operands.append(acc)
        if last:
            shape = (n_pair, part_rows, d)
            out_specs += [whole_spec(shape)] * (2 * n_part)
            out_shape += [jax.ShapeDtypeStruct(shape, t) for t in (BF16, F32) for _ in range(n_part)]
            scratch.append(pltpu.VMEM((tokens, d), F32))
        else:
            out_specs.append(whole_spec((tokens, d)))
            out_shape.append(jax.ShapeDtypeStruct((tokens, d), F32))
    if with_weight:
        if grads is not None:
            for k, e in enumerate(grads):
                aliases[4 + len(operands)] = len(out_shape) + k
                in_specs.append(ANY)
                operands.append(e)
        out_specs += [cols_spec(d, first), cols_spec(d, first), rows_spec(d, first)]
        out_shape += [jax.ShapeDtypeStruct(s, BF16) for s in ((d, ff), (d, ff), (ff, d))]
    in_specs += [ANY] * len(deps)
    operands += deps
    width = tiles * TILE
    outs = pl.pallas_call(
        kernel,
        grid_spec=pltpu.PrefetchScalarGridSpec(
            num_scalar_prefetch=4,
            grid=(tiles,),
            in_specs=in_specs,
            out_specs=out_specs,
            scratch_shapes=scratch,
        ),
        out_shape=out_shape,
        input_output_aliases=aliases,
        compiler_params=params(),
        cost_estimate=cost("B" if len(wanted) == 2 else wanted[0][0].upper(), tiles),
        name="backward_" + "_".join(wanted) + f"_t{tiles}",
    )(jnp.zeros((1,), jnp.int32) if x_index is None else x_index, *masks, *operands)
    n_in = (2 * n_part if last else 1) if with_input else 0
    return outs[:n_in], outs[n_in:]


def local_grads(sums):
    gate_sum, up_sum, back_sum = sums[:, 0], sums[:, 1], sums[:, 2]
    sigmoid_gate = jax.nn.sigmoid(gate_sum)
    silu = gate_sum * sigmoid_gate
    hidden = silu * up_sum
    slope = sigmoid_gate * (1.0 + gate_sum * (1.0 - sigmoid_gate))
    return tuple(v.astype(BF16) for v in (hidden, back_sum * up_sum * slope, back_sum * silu))


def after(token, *arrays):
    return lax.optimization_barrier((*arrays, token))[: len(arrays)]


def plan(tiles):
    if tiles < 14:
        sizes = [1, 2, tiles - 3]
        pieces = [(0, 0, 1), (1, 0, 2), (2, 0, tiles - 3)]
        steps = (
        "F0", "F1", "S0", "F2", "S1", "L0", "S2", "L1", "I0,1", "L2", "E2", "W0,1", "X0", "W2",
    )
        return sizes, pieces, steps, 1
    sizes = [1, 2, 3, 3, 3, 2]
    pieces = [(0, 0, 1), (1, 0, 2), (2, 0, 3), (3, 0, 3), (4, 0, 3), (5, 0, 2)]
    steps = (
        "F0", "S0", "F1", "S1", "F2", "F3", "L0", "S2", "F4", "L1", "S3", "F5", "I0,1", "L2", "S4", "W0,1",
        "I2", "L3", "S5", "I3", "L4", "I4", "L5", "E5", "W2", "X0", "W3", "X1", "W4,5",
    )
    return sizes, pieces, steps, 2


def build(n_row, n_col):
    n_y = n_row // 2
    n_pair = n_col // 2

    def swap_core(v):
        return lax.ppermute(v, "row", [(i, i ^ 1) for i in range(n_row)])

    def from_y(v):
        return [
            lax.ppermute(v, "row", [(i, (i + 2 * s) % n_row) for i in range(n_row)]) for s in range(1, n_y)
        ]

    def shards(inputs, out_grad, gate_w, up_w, down_w, gate_mask, up_mask, down_mask):
        ff = gate_w.shape[1]
        core_arg = (lax.axis_index("row") % 2).reshape(1).astype(jnp.int32)
        col = lax.axis_index("col")
        x_pos, z_pos = col % 2, col // 2
        flip = core_arg[0] * (n_pair // 2)
        x_arg = x_pos.reshape(1).astype(jnp.int32)
        masks = (gate_mask, up_mask, down_mask)
        weights = [gate_w, up_w, down_w]
        sizes, pieces, steps, n_part = plan(ff // TILE)
        firsts = [sum(sizes[:c]) for c in range(len(sizes))]
        kept, crossed = {}, {}
        mine, arrived, values = {}, {}, {}
        acc, grads = None, None
        token, parts = None, []
        x, g = inputs, out_grad

        for step in steps:
            kind, what = step[0], [int(k) for k in step[1:].split(",")]
            if kind not in "BIEW":
                what = what[0]
            deps = [] if token is None else [token]
            if kind == "F":
                arrange = not kept
                kept[what], *rest = forward(
                    core_arg, x, g, weights, masks, firsts[what], sizes[what], n_pair, deps, arrange
                )
                if arrange:
                    x, g = rest[3:]
                crossed[what] = [swap_core(v) for v in rest[:3]]
                token = kept[what]
            elif kind == "S":
                c, at, size = pieces[what]
                keep, *cross = after(token, kept[c], *crossed[c])
                mine[what] = keep[at : at + size] + jnp.stack([v[at : at + size] for v in cross], axis=1).astype(F32)
                sent = mine[what].astype(BF16)
                arrived[what] = from_y(sent)
                token = sent
            elif kind == "L":
                total, *others = after(token, mine[what], *arrived[what])
                for other in others:
                    total = total + other.astype(F32)
                own = local_grads(total)
                values[what] = (own, tuple(swap_core(v) for v in own))
                token = own[2]
            elif kind == "X":
                keep, cross = after(token, keeps[what], from_x[what])
                summed = keep + cross.astype(F32)
                token = lax.dynamic_index_in_dim(summed, z_pos ^ flip, 0, keepdims=False)
                from_z = []
                for s in range(1, n_pair):
                    out = lax.dynamic_index_in_dim(summed, (z_pos ^ s) ^ flip, 0, keepdims=False).astype(BF16)
                    from_z.append(lax.ppermute(out, "col", [(j, j ^ (2 * s)) for j in range(n_col)]))
                parts.append((token, from_z))
            else:
                wanted = {"B": ("input", "weight"), "I": ("input",), "E": ("input",), "W": ("weight",)}[kind]
                c, at, _ = pieces[what[0]]
                part, new = backward(
                    [values[i] for i in what],
                    x,
                    g,
                    weights,
                    masks,
                    firsts[c] + at,
                    acc,
                    grads,
                    x_arg if kind == "E" else None,
                    wanted,
                    n_col,
                    deps,
                    n_part,
                )
                if new:
                    grads = new
                if kind == "E":
                    gives, keeps = part[:n_part], part[n_part:]
                    from_x = [lax.ppermute(v, "col", [(j, j ^ 1) for j in range(n_col)]) for v in gives]
                elif part:
                    acc = part[0]
                token = new[0] if new else part[0]

        rows = []
        for own, from_z in parts:
            total, *from_z = after(token, own, *from_z)
            for v in from_z:
                total = total + v.astype(F32)
            rows.append(total.astype(BF16))
        return (jnp.concatenate(rows, axis=0), *grads)

    return shards


def solution(mesh):
    placed = (
        P(None, "row"),
        P(None, "row"),
        P("row", "col"),
        P("row", "col"),
        P("col", "row"),
        P("row", "col"),
        P("row", "col"),
        P("col", "row"),
    )
    return jax.shard_map(
        build(mesh.shape["row"], mesh.shape["col"]),
        mesh=mesh,
        in_specs=placed,
        out_specs=(P("col", "row"), P("row", "col"), P("row", "col"), P("col", "row")),
        check_vma=False,
    )
```

time: 249 us -> 221 us (0.89)
  waiting for transfers between devices: 58.4 us -> 21.9 us
  Pallas kernels: 150 us -> 130 us
  local copies, waits for them, and re-layouts: 6.23 us -> 21.5 us
  starting transfers between devices: 12.5 us -> 24 us
    ppermute x4 -> x8, waiting for transfers between devices: 38 us -> 4.72 us  [the longest x6 4.71 us: shards(): lax.ppermute(out, 'col', [(j, j ^ 2 * s) for j in range(n_col)])]
    unnamed x27 -> x83, local copies, waits for them, and re-layouts: 6.12 us -> 17 us
    pallas_call x6 -> x9, Pallas kernels: 92.6 us -> 82.3 us  [backward(): pl.pallas_call(kernel, grid_spec=pltpu.PrefetchScalarGridSpec(num_scalar_...]
    pallas_call x6, Pallas kernels: 57.5 us -> 47.8 us  [forward(): pl.pallas_call(kernel, grid_spec=pltpu.PrefetchScalarGridSpec(num_scalar_...]
    ppermute x13 -> x36, starting transfers between devices: 2.73 us -> 8.91 us  [swap_core(): return lax.ppermute(v, 'row', [(i, i ^ 1) for i in range(n_row)])]
    ppermute x4 -> x8, starting transfers between devices: 4.07 us -> 9.85 us  [the longest x6 7.83 us: shards(): lax.ppermute(out, 'col', [(j, j ^ 2 * s) for j in range(n_col)])]
    convert_element_type x1 -> x7, local copies, waits for them, and re-layouts: 0.11 us -> 4.47 us  [the longest x5 4.37 us: shards(): sent = mine[what].astype(BF16)]
    convert_element_type x1 -> x7, other arithmetic: 1.77 us -> 5.52 us  [the longest x6 5.39 us: local_grads(): v.astype(BF16)]
  transfers between devices with their start and end apart: 24 -> 50, of which waited for: 14 -> 17; matrix products, arithmetic and copies ran while one was open for 5% -> 9% of each run, Pallas kernels for 50% -> 51%
where the time goes in v2:
time: 221 us; the launch traced here: 217 us
  Pallas kernels  130 us (59%)
  starting transfers between devices  24 us (11%)
  waiting for transfers between devices  21.9 us (10%)
  local copies, waits for them, and re-layouts  21.5 us (10%)
  other arithmetic  17.4 us (8%)
    pallas_call x9, Pallas kernels, backward(): pl.pallas_call(kernel, grid_spec=pltpu.PrefetchScalarGridSpec(num_scalar_...  82.3 us
    pallas_call x6, Pallas kernels, forward(): pl.pallas_call(kernel, grid_spec=pltpu.PrefetchScalarGridSpec(num_scalar_...  47.8 us
    unnamed x83, local copies, waits for them, and re-layouts  17 us
    ppermute x6, waiting for transfers between devices, from_y(): lax.ppermute(v, 'row', [(i, (i + 2 * s) % n_row) for i in range(n_row)])  8.94 us
    ppermute x36, starting transfers between devices, swap_core(): return lax.ppermute(v, 'row', [(i, i ^ 1) for i in range(n_row)])  8.91 us
    ppermute x36, waiting for transfers between devices, swap_core(): return lax.ppermute(v, 'row', [(i, i ^ 1) for i in range(n_row)])  8.23 us
    ppermute x6, starting transfers between devices, shards(): lax.ppermute(out, 'col', [(j, j ^ 2 * s) for j in range(n_col)])  7.83 us
    convert_element_type x6, other arithmetic, shards(): sent = mine[what].astype(BF16)  6.73 us
  transfers between devices with their start and end apart: 50, of which 17 were waited for; matrix products, arithmetic and copies ran while one was open for 9% of the time, Pallas kernels for 51%

profile of v2, /device:TPU:14, one launch (start us, length us, event | category | flops | bytes accessed | tf_op | source)
XLA Modules:
  0.0 216.5 jit_solution(3998957894816074677)
XLA Ops:
  1.4 1.6 copy-done.10
  3.0 1.6 copy-done.11
  6.0 5.1 %forward_t1.1 = (f32[1,3,4,64,256]{4,3,2,1,0:T(8,128)S(1)}, bf16[1,4,64,256]{3,2,1,0:T(8,128)(2,1)S(1)}, bf16[1,4,64,256]{3,2,1,0:T(8,128)(2,1)S(1)}, bf16[1,4,6...) custom-call(s32[1]{0:T(128)} %bitcast.1.core_ref, ...), custom_call_target="tpu_custom_call" | custom-call | flops 8400000 | tf_op jit(solution)/shard_map/forward_t1/pallas_call | solution.py:84
  13.2 7.4 %forward_t2.2 = (f32[2,3,4,64,256]{4,3,2,1,0:T(8,128)S(1)}, bf16[2,4,64,256]{3,2,1,0:T(8,128)(2,1)S(1)}, bf16[2,4,64,256]{3,2,1,0:T(8,128)(2,1)S(1)}, bf16[2,4,64,256]{3,2,1,0:T(8,128)(2,1)S(1)}) custom-call(s32[1]{0:T(128)} %bitcast.1.core_ref, s32[16,28]{1,0:T(8,128)S(1)} %copy-done.12, s32[16,28]{1,0:T(8,128)S(1)} %copy-done.16, s32[28,16]{1,0:T(8,128)S(1)} %copy.42.dm, ...), custom_call_target="tpu_custom_call" | custom-call | flops 16800000 | tf_op jit(solution)/shard_map/forward_t2/pallas_call | solution.py:84
  23.9 9.3 %forward_t3.3 = (f32[3,3,4,64,256]{4,3,2,1,0:T(8,128)S(1)}, bf16[3,4,64,256]{3,2,1,0:T(8,128)(2,1)S(1)}, bf16[3,4,64,256]{3,2,1,0:T(8,128)(2,1)S(1)}, bf16[3,4,64,256]{3,2,1,0:T(8,128)(2,1)S(1)}) custom-call(s32[1]{0:T(128)} %bitcast.1.core_ref, s32[16,28]{1,0:T(8,128)S(1)} %copy-done.12, s32[16,28]{1,0:T(8,128)S(1)} %copy-done.16, s32[28,16]{1,0:T(8,128)S(1)} %copy.42.dm, ...), custom_call_target="tpu_custom_call" | custom-call | flops 25200000 | tf_op jit(solution)/shard_map/forward_t3/pallas_call | solution.py:84
  33.9 9.3 %forward_t3.4 = (f32[3,3,4,64,256]{4,3,2,1,0:T(8,128)S(1)}, bf16[3,4,64,256]{3,2,1,0:T(8,128)(2,1)S(1)}, bf16[3,4,64,256]{3,2,1,0:T(8,128)(2,1)S(1)}, bf16[3,4,64,256]{3,2,1,0:T(8,128)(2,1)S(1)}) custom-call(s32[1]{0:T(128)} %bitcast.1.core_ref, s32[16,28]{1,0:T(8,128)S(1)} %copy-done.12, s32[16,28]{1,0:T(8,128)S(1)} %copy-done.16, s32[28,16]{1,0:T(8,128)S(1)} %copy.42.dm, ...), custom_call_target="tpu_custom_call" | custom-call | flops 25200000 | tf_op jit(solution)/shard_map/forward_t3/pallas_call | solution.py:84
  43.5 1.5 fusion.15
  48.7 9.4 %forward_t3.5 = (f32[3,3,4,64,256]{4,3,2,1,0:T(8,128)S(1)}, bf16[3,4,64,256]{3,2,1,0:T(8,128)(2,1)S(1)}, bf16[3,4,64,256]{3,2,1,0:T(8,128)(2,1)S(1)}, bf16[3,4,64,256]{3,2,1,0:T(8,128)(2,1)S(1)}) custom-call(s32[1]{0:T(128)} %bitcast.1.core_ref, s32[16,28]{1,0:T(8,128)S(1)} %copy-done.12, s32[16,28]{1,0:T(8,128)S(1)} %copy-done.16, s32[28,16]{1,0:T(8,128)S(1)} %copy.42.dm, ...), custom_call_target="tpu_custom_call" | custom-call | flops 25200000 | tf_op jit(solution)/shard_map/forward_t3/pallas_call | solution.py:84
  59.8 2.2 %fusion.14 = (bf16[3,3,4,64,256]{4,3,2,0,1:T(8,128)(2,1)}, f32[3,3,4,64,256]{4,3,2,0,1:T(8,128)}) fusion(bf16[3,1,4,64,256]{4,3,2,0,1:T(8,128)(2,1)S(1)} %bitcast.171, bf16[3,1,4,64,256]{4,3,2,0,1:T(8,128)(2,1)S(1)} %bitcast.169, bf16[3,1,4,64,256]{4,3,2,0,1:T(8,128)(2,1)S(1)} %bitcast.168, f32[3,3,4,64,256]{4,3,2,1,0:T(8,128)S(1)} %get-tuple-element.129), kind=kLoop, calls=%fused_computation.81 | loop fusion | flops 2949120 | bytes 7077888 | tf_op jit(solution)/shard_map/convert_element_type | solution.py:325
  64.0 7.2 %forward_t2.3 = (f32[2,3,4,64,256]{4,3,2,1,0:T(8,128)S(1)}, bf16[2,4,64,256]{3,2,1,0:T(8,128)(2,1)S(1)}, bf16[2,4,64,256]{3,2,1,0:T(8,128)(2,1)S(1)}, bf16[2,4,64,256]{3,2,1,0:T(8,128)(2,1)S(1)}) custom-call(s32[1]{0:T(128)} %bitcast.1.core_ref, s32[16,28]{1,0:T(8,128)S(1)} %copy-done.12, s32[16,28]{1,0:T(8,128)S(1)} %copy-done.16, s32[28,16]{1,0:T(8,128)S(1)} %copy.42.dm, ...), custom_call_target="tpu_custom_call" | custom-call | flops 16800000 | tf_op jit(solution)/shard_map/forward_t2/pallas_call | solution.py:84
  71.9 8.8 %backward_input_t3.4.refs_6_ = f32[512,2048]{1,0:T(8,128)S(1)} custom-call(s32[1]{0:T(128)} %constant.60.clone.1.xi, s32[16,28]{1,0:T(8,128)S(1)} %copy-done.13, s32[16,28]{1,0:T(8,128)S(1)} %copy-done.16, s32[28,16]{1,0:T(8,128)S(1)} %copy.42.dm, bf16[1,4,64,256]{3,2,1,0:T(8,128)(2,1)S(1)} %get-tuple-element.218.refs_0_.refs_1_, ...), custom_call_target="tpu_custom_call" | custom-call | flops 25200000 | tf_op jit(solution)/shard_map/backward_input_t3/pallas_call | solution.py:229
  81.2 1.6 convert_add_fusion.2
  84.8 2.3 %fusion.13 = (bf16[3,3,4,64,256]{4,3,2,0,1:T(8,128)(2,1)}, f32[3,3,4,64,256]{4,3,2,0,1:T(8,128)}) fusion(bf16[3,1,4,64,256]{4,3,2,0,1:T(8,128)(2,1)S(1)} %bitcast.175, bf16[3,1,4,64,256]{4,3,2,0,1:T(8,128)(2,1)S(1)} %bitcast.172, bf16[3,1,4,64,256]{4,3,2,0,1:T(8,128)(2,1)S(1)} %bitcast.170, f32[3,3,4,64,256]{4,3,2,1,0:T(8,128)S(1)} %get-tuple-element.142), kind=kLoop, calls=%fused_computation.80 | loop fusion | flops 2949120 | bytes 7077888 | tf_op jit(solution)/shard_map/convert_element_type | solution.py:325
  87.0 1.5 collective-permute-start.31
  90.2 8.4 %backward_weight_t3.3 = (bf16[2048,3584]{1,0:T(8,128)(2,1)}, bf16[2048,3584]{1,0:T(8,128)(2,1)}, bf16[3584,2048]{1,0:T(8,128)(2,1)}) custom-call(s32[1]{0:T(128)} %constant.60.clone.1.xi, s32[16,28]{1,0:T(8,128)S(1)} %copy-done.13, s32[16,28]{1,0:T(8,128)S(1)} %copy-done.16, s32[28,16]{1,0:T(8,128)S(1)} %copy.42.dm, ...), custom_call_target="tpu_custom_call" | custom-call | flops 25200000 | tf_op jit(solution)/shard_map/backward_weight_t3/pallas_call | solution.py:229
  99.1 8.6 %backward_input_t3.5.refs_6_ = f32[512,2048]{1,0:T(8,128)S(1)} custom-call(s32[1]{0:T(128)} %constant.60.clone.1.xi, s32[16,28]{1,0:T(8,128)S(1)} %copy-done.13, s32[16,28]{1,0:T(8,128)S(1)} %copy-done.16, s32[28,16]{1,0:T(8,128)S(1)} %copy.42.dm, bf16[3,4,64,256]{3,2,1,0:T(8,128)(2,1)S(1)} %get-tuple-element.201.refs_0_.refs_1_, ...), custom_call_target="tpu_custom_call" | custom-call | flops 25200000 | tf_op jit(solution)/shard_map/backward_input_t3/pallas_call | solution.py:229
  111.8 8.6 %backward_input_t3.6.refs_6_ = f32[512,2048]{1,0:T(8,128)S(1)} custom-call(s32[1]{0:T(128)} %constant.60.clone.1.xi, s32[16,28]{1,0:T(8,128)S(1)} %copy-done.13, s32[16,28]{1,0:T(8,128)S(1)} %copy-done.16, s32[28,16]{1,0:T(8,128)S(1)} %copy.42.dm, bf16[3,4,64,256]{3,2,1,0:T(8,128)(2,1)S(1)} %get-tuple-element.203.refs_0_.refs_1_, ...), custom_call_target="tpu_custom_call" | custom-call | flops 25200000 | tf_op jit(solution)/shard_map/backward_input_t3/pallas_call | solution.py:229
  120.4 5.6 %collective-permute-done.31 = bf16[3,3,4,64,256]{4,3,2,0,1:T(8,128)(2,1)S(1)} collective-permute-done((bf16[3,3,4,64,256]{4,3,2,0,1:T(8,128)(2,1)}, bf16[3,3,4,64,256]{4,3,2,0,1:T(8,128)(2,1)S(1)}, u32[]{:S(2)}, u32[]{:S(2)}) %collective-permute-start.31) | collective-permute-done | bytes 1179680 | tf_op jit(solution)/shard_map/ppermute | solution.py:287
  130.0 8.9 %backward_input_t3.7.refs_6_ = f32[512,2048]{1,0:T(8,128)S(1)} custom-call(s32[1]{0:T(128)} %constant.60.clone.1.xi, s32[16,28]{1,0:T(8,128)S(1)} %copy-done.13, s32[16,28]{1,0:T(8,128)S(1)} %copy-done.16, s32[28,16]{1,0:T(8,128)S(1)} %copy.42.dm, bf16[3,4,64,256]{3,2,1,0:T(8,128)(2,1)S(1)} %get-tuple-element.198.refs_0_.refs_1_, ...), custom_call_target="tpu_custom_call" | custom-call | flops 25200000 | tf_op jit(solution)/shard_map/backward_input_t3/pallas_call | solution.py:229
  138.9 3.4 %collective-permute-done.30 = bf16[2,3,4,64,256]{4,3,2,0,1:T(8,128)(2,1)S(1)} collective-permute-done((bf16[2,3,4,64,256]{4,3,2,0,1:T(8,128)(2,1)S(1)}, bf16[2,3,4,64,256]{4,3,2,0,1:T(8,128)(2,1)S(1)}, u32[]{:S(2)}, u32[]{:S(2)}) %collective-permute-start.30) | collective-permute-done | bytes 786464 | tf_op jit(solution)/shard_map/ppermute | solution.py:287
  144.1 1.7 collective-permute-done.36.refs_2_.refs_10_
  145.8 2.2 %copy-done.3 = f32[512,2048]{1,0:T(8,128)S(1)} copy-done((f32[512,2048]{1,0:T(8,128)S(1)}, f32[512,2048]{1,0:T(8,128)}, u32[]{:S(2)}) %copy-start.3) | copy-done | bytes 4194328
  149.4 7.7 %backward_input_t2.1 = (bf16[4,32,2048]{2,1,0:T(8,128)(2,1)}, bf16[4,32,2048]{2,1,0:T(8,128)(2,1)S(1)}, f32[4,32,2048]{2,1,0:T(8,128)S(1)}, f32[4,32,2048]{2,1,0:T(8,128)S(1)}) custom-call(s32[1]{0:T(128)} %bitcast.xi, s32[16,28]{1,0:T(8,128)S(1)} %copy-done.14, s32[16,28]{1,0:T(8,128)S(1)} %copy-done.17, s32[28,16]{1,0:T(8,128)S(1)} %copy.42.dm, ...), custom_call_target="tpu_custom_call" | custom-call | flops 16800000 | tf_op jit(solution)/shard_map/backward_input_t2/pallas_call | solution.py:229
  161.5 1.6 collective-permute-done.39.refs_3_
  164.5 1.6 copy-done.1
  169.5 9.4 %backward_weight_t3.4 = (bf16[2048,3584]{1,0:T(8,128)(2,1)}, bf16[2048,3584]{1,0:T(8,128)(2,1)}, bf16[3584,2048]{1,0:T(8,128)(2,1)}) custom-call(s32[1]{0:T(128)} %constant.60.clone.1.xi, s32[16,28]{1,0:T(8,128)S(1)} %copy-done.15, s32[16,28]{1,0:T(8,128)S(1)} %copy-done.18, ...), custom_call_target="tpu_custom_call", output_to_operand_aliasing={{0}: (12, {}), {1}: (13, {}), {2}: (14, {})} | custom-call | flops 25200000 | tf_op jit(solution)/shard_map/backward_weight_t3/pallas_call | solution.py:229
  180.5 8.4 %backward_weight_t3.5 = (bf16[2048,3584]{1,0:T(8,128)(2,1)}, bf16[2048,3584]{1,0:T(8,128)(2,1)}, bf16[3584,2048]{1,0:T(8,128)(2,1)}) custom-call(s32[1]{0:T(128)} %constant.60.clone.1.xi, s32[16,28]{1,0:T(8,128)S(1)} %copy-done.15, s32[16,28]{1,0:T(8,128)S(1)} %copy-done.18, ...), custom_call_target="tpu_custom_call", output_to_operand_aliasing={{0}: (12, {}), {1}: (13, {}), {2}: (14, {})} | custom-call | flops 25200000 | tf_op jit(solution)/shard_map/backward_weight_t3/pallas_call | solution.py:229
  189.5 2.6 %collective-permute-start.41 = (bf16[32,2048]{1,0:T(8,128)(2,1)S(1)}, bf16[32,2048]{1,0:T(8,128)(2,1)S(1)}, u32[]{:S(2)}, u32[]{:S(2)}) collective-permute-start(bf16[32,2048]{1,0:T(8,128)(2,1)S(1)} %get-tuple-element.212), channel_id=1, source_target_pairs={{0,4},{1,5},{2,6},{3,7},{4,0},{5,1},{6,2},{7,3},{8,12},{9,13},{10,... | collective-permute-start | bytes 393224 | tf_op jit(solution)/shard_map/ppermute | solution.py:342
  194.2 2.2 %collective-permute-start.48 = (bf16[32,2048]{1,0:T(8,128)(2,1)S(1)}, bf16[32,2048]{1,0:T(8,128)(2,1)S(1)}, u32[]{:S(2)}, u32[]{:S(2)}) collective-permute-start(bf16[32,2048]{1,0:T(8,128)(2,1)S(1)} %get-tuple-element.215), channel_id=1, source_target_pairs={{0,4},{1,5},{2,6},{3,7},{4,0},{5,1},{6,2},{7,3},{8,12},{9,13},{10,... | collective-permute-start | bytes 393224 | tf_op jit(solution)/shard_map/ppermute | solution.py:342
  197.1 13.4 %backward_weight_t5.1 = (bf16[2048,3584]{1,0:T(8,128)(2,1)}, bf16[2048,3584]{1,0:T(8,128)(2,1)}, bf16[3584,2048]{1,0:T(8,128)(2,1)}) custom-call(s32[1]{0:T(128)} %constant.60.clone.1.xi, s32[16,28]{1,0:T(8,128)S(1)} %copy-done.15, s32[16,28]{1,0:T(8,128)S(1)} %copy-done.18, ...), custom_call_target="tpu_custom_call", output_to_operand_aliasing={{0}: (18, {}), {1}: (19, {}), {2}: (20, {})} | custom-call | flops 42000000 | tf_op jit(solution)/shard_map/backward_weight_t5/pallas_call | solution.py:229
  211.0 1.8 collective-permute-done.48
  212.8 2.4 %collective-permute-done.49 = bf16[32,2048]{1,0:T(8,128)(2,1)S(1)} collective-permute-done((bf16[32,2048]{1,0:T(8,128)(2,1)S(1)}, bf16[32,2048]{1,0:T(8,128)(2,1)S(1)}, u32[]{:S(2)}, u32[]{:S(2)}) %collective-permute-start.49) | collective-permute-done | bytes 131104 | tf_op jit(solution)/shard_map/ppermute | solution.py:342
  (197 shorter events, 47.4 us)
Async XLA Ops:
  21.3 21.9 %collective-permute-start.13 = (bf16[1,3,4,64,256]{4,3,2,1,0:T(8,128)(2,1)S(1)}, bf16[1,3,4,64,256]{4,3,2,1,0:T(8,128)(2,1)S(1)}, u32[]{:S(2)}, u32[]{:S(2)}) collective-permute-start(bf16[1,3,4,64,256]{4,3,2,1,0:T(8,128)(2,1)S(1)} %get-tuple-element.194.rest_0_), channel_id=1, source_target_pairs={{0,16},{8,24},{16,0},{24,8},{1,17},{9,25},{17,1},{25,9},{2,18},{10... | collective-permute-start | bytes 1179656 | tf_op jit(solution)/shard_map/ppermute | solution.py:287
  23.3 34.7 %collective-permute-start.9 = (bf16[2,3,4,64,256]{4,3,2,0,1:T(8,128)(2,1)S(1)}, bf16[2,3,4,64,256]{4,3,2,0,1:T(8,128)(2,1)S(1)}, u32[]{:S(2)}, u32[]{:S(2)}) collective-permute-start(bf16[2,3,4,64,256]{4,3,2,0,1:T(8,128)(2,1)S(1)} %get-tuple-element.192), channel_id=1, source_target_pairs={{0,16},{8,24},{16,0},{24,8},{1,17},{9,25},{17,1},{25,9},{2,18},{10... | collective-permute-start | bytes 2359304 | tf_op jit(solution)/shard_map/ppermute | solution.py:287
  33.2 10.3 %collective-permute-start.10 = (bf16[3,4,64,256]{3,2,1,0:T(8,128)(2,1)S(1)}, bf16[3,4,64,256]{3,2,1,0:T(8,128)(2,1)S(1)}, u32[]{:S(2)}, u32[]{:S(2)}) collective-permute-start(bf16[3,4,64,256]{3,2,1,0:T(8,128)(2,1)S(1)} %get-tuple-element.117), channel_id=1, source_target_pairs={{0,8},{8,0},{16,24},{24,16},{1,9},{9,1},{17,25},{25,17},{2,10},{10... | collective-permute-start | bytes 1179656 | tf_op jit(solution)/shard_map/ppermute | solution.py:283
  33.3 10.2 %collective-permute-start.11 = (bf16[3,4,64,256]{3,2,1,0:T(8,128)(2,1)S(1)}, bf16[3,4,64,256]{3,2,1,0:T(8,128)(2,1)S(1)}, u32[]{:S(2)}, u32[]{:S(2)}) collective-permute-start(bf16[3,4,64,256]{3,2,1,0:T(8,128)(2,1)S(1)} %get-tuple-element.118), channel_id=1, source_target_pairs={{0,8},{8,0},{16,24},{24,16},{1,9},{9,1},{17,25},{25,17},{2,10},{10... | collective-permute-start | bytes 1179656 | tf_op jit(solution)/shard_map/ppermute | solution.py:283
  45.1 35.7 %collective-permute-start.18 = (bf16[3,3,4,64,256]{4,3,2,0,1:T(8,128)(2,1)}, bf16[3,3,4,64,256]{4,3,2,0,1:T(8,128)(2,1)}, u32[]{:S(2)}, u32[]{:S(2)}) collective-permute-start(bf16[3,3,4,64,256]{4,3,2,0,1:T(8,128)(2,1)} %get-tuple-element.190), channel_id=1, source_target_pairs={{0,16},{8,24},{16,0},{24,8},{1,17},{9,25},{17,1},{25,9},{2,18},{10... | collective-permute-start | bytes 3538952 | tf_op jit(solution)/shard_map/ppermute | solution.py:287
  46.6 12.4 %collective-permute-start.6 = (bf16[3,4,64,256]{3,2,1,0:T(8,128)(2,1)S(1)}, bf16[3,4,64,256]{3,2,1,0:T(8,128)(2,1)S(1)}, u32[]{:S(2)}, u32[]{:S(2)}) collective-permute-start(bf16[3,4,64,256]{3,2,1,0:T(8,128)(2,1)S(1)} %get-tuple-element.114), channel_id=1, source_target_pairs={{0,8},{8,0},{16,24},{24,16},{1,9},{9,1},{17,25},{25,17},{2,10},{10... | collective-permute-start | bytes 1179656 | tf_op jit(solution)/shard_map/ppermute | solution.py:283
  46.8 12.5 %collective-permute-start.7 = (bf16[3,4,64,256]{3,2,1,0:T(8,128)(2,1)S(1)}, bf16[3,4,64,256]{3,2,1,0:T(8,128)(2,1)S(1)}, u32[]{:S(2)}, u32[]{:S(2)}) collective-permute-start(bf16[3,4,64,256]{3,2,1,0:T(8,128)(2,1)S(1)} %get-tuple-element.115), channel_id=1, source_target_pairs={{0,8},{8,0},{16,24},{24,16},{1,9},{9,1},{17,25},{25,17},{2,10},{10... | collective-permute-start | bytes 1179656 | tf_op jit(solution)/shard_map/ppermute | solution.py:283
  47.1 12.5 %collective-permute-start.8 = (bf16[3,4,64,256]{3,2,1,0:T(8,128)(2,1)S(1)}, bf16[3,4,64,256]{3,2,1,0:T(8,128)(2,1)S(1)}, u32[]{:S(2)}, u32[]{:S(2)}) collective-permute-start(bf16[3,4,64,256]{3,2,1,0:T(8,128)(2,1)S(1)} %get-tuple-element.116), channel_id=1, source_target_pairs={{0,8},{8,0},{16,24},{24,16},{1,9},{9,1},{17,25},{25,17},{2,10},{10... | collective-permute-start | bytes 1179656 | tf_op jit(solution)/shard_map/ppermute | solution.py:283
  58.0 13.2 %collective-permute-start.20 = (bf16[1,4,64,256]{3,2,1,0:T(8,128)(2,1)S(1)}, bf16[1,4,64,256]{3,2,1,0:T(8,128)(2,1)S(1)}, u32[]{:S(2)}, u32[]{:S(2)}) collective-permute-start(bf16[1,4,64,256]{3,2,1,0:T(8,128)(2,1)S(1)} %get-tuple-element.219.refs_1_.refs_2_), channel_id=1, source_target_pairs={{0,8},{8,0},{16,24},{24,16},{1,9},{9,1},{17,25},{25,17},{2,10},{10... | collective-permute-start | bytes 393224 | tf_op jit(solution)/shard_map/ppermute | solution.py:283
  59.3 12.5 %collective-permute-start.22 = (bf16[2,4,64,256]{3,2,1,0:T(8,128)(2,1)S(1)}, bf16[2,4,64,256]{3,2,1,0:T(8,128)(2,1)S(1)}, u32[]{:S(2)}, u32[]{:S(2)}) collective-permute-start(bf16[2,4,64,256]{3,2,1,0:T(8,128)(2,1)S(1)} %get-tuple-element.210.refs_5_.refs_8_), channel_id=1, source_target_pairs={{0,8},{8,0},{16,24},{24,16},{1,9},{9,1},{17,25},{25,17},{2,10},{10... | collective-permute-start | bytes 786440 | tf_op jit(solution)/shard_map/ppermute | solution.py:283
  59.6 11.7 %collective-permute-start.21 = (bf16[2,4,64,256]{3,2,1,0:T(8,128)(2,1)S(1)}, bf16[2,4,64,256]{3,2,1,0:T(8,128)(2,1)S(1)}, u32[]{:S(2)}, u32[]{:S(2)}) collective-permute-start(bf16[2,4,64,256]{3,2,1,0:T(8,128)(2,1)S(1)} %get-tuple-element.209.refs_4_.refs_7_), channel_id=1, source_target_pairs={{0,8},{8,0},{16,24},{24,16},{1,9},{9,1},{17,25},{25,17},{2,10},{10... | collective-permute-start | bytes 786440 | tf_op jit(solution)/shard_map/ppermute | solution.py:283
  62.0 45.8 %collective-permute-start.17 = (bf16[3,3,4,64,256]{4,3,2,0,1:T(8,128)(2,1)}, bf16[3,3,4,64,256]{4,3,2,0,1:T(8,128)(2,1)S(1)}, u32[]{:S(2)}, u32[]{:S(2)}) collective-permute-start(bf16[3,3,4,64,256]{4,3,2,0,1:T(8,128)(2,1)} %get-tuple-element.188), channel_id=1, source_target_pairs={{0,16},{8,24},{16,0},{24,8},{1,17},{9,25},{17,1},{25,9},{2,18},{10... | collective-permute-start | bytes 3538952 | tf_op jit(solution)/shard_map/ppermute | solution.py:287
  71.2 15.8 %collective-permute-start.25 = (bf16[1,4,64,256]{3,2,1,0:T(8,128)(2,1)S(1)}, bf16[1,4,64,256]{3,2,1,0:T(8,128)(2,1)S(1)}, u32[]{:S(2)}, u32[]{:S(2)}) collective-permute-start(bf16[1,4,64,256]{3,2,1,0:T(8,128)(2,1)S(1)} %get-tuple-element.217.refs_0_), channel_id=1, source_target_pairs={{0,8},{8,0},{16,24},{24,16},{1,9},{9,1},{17,25},{25,17},{2,10},{10... | collective-permute-start | bytes 393224 | tf_op jit(solution)/shard_map/ppermute | solution.py:283
  71.3 12.8 %collective-permute-start.27 = (bf16[3,4,64,256]{3,2,1,0:T(8,128)(2,1)S(1)}, bf16[3,4,64,256]{3,2,1,0:T(8,128)(2,1)S(1)}, u32[]{:S(2)}, u32[]{:S(2)}) collective-permute-start(bf16[3,4,64,256]{3,2,1,0:T(8,128)(2,1)S(1)} %get-tuple-element.139), channel_id=1, source_target_pairs={{0,8},{8,0},{16,24},{24,16},{1,9},{9,1},{17,25},{25,17},{2,10},{10... | collective-permute-start | bytes 1179656 | tf_op jit(solution)/shard_map/ppermute | solution.py:283
  71.8 12.4 %collective-permute-start.28 = (bf16[3,4,64,256]{3,2,1,0:T(8,128)(2,1)S(1)}, bf16[3,4,64,256]{3,2,1,0:T(8,128)(2,1)S(1)}, u32[]{:S(2)}, u32[]{:S(2)}) collective-permute-start(bf16[3,4,64,256]{3,2,1,0:T(8,128)(2,1)S(1)} %get-tuple-element.140), channel_id=1, source_target_pairs={{0,8},{8,0},{16,24},{24,16},{1,9},{9,1},{17,25},{25,17},{2,10},{10... | collective-permute-start | bytes 1179656 | tf_op jit(solution)/shard_map/ppermute | solution.py:283
  84.2 14.7 %collective-permute-start.24 = (bf16[3,4,64,256]{3,2,1,0:T(8,128)(2,1)S(1)}, bf16[3,4,64,256]{3,2,1,0:T(8,128)(2,1)S(1)}, u32[]{:S(2)}, u32[]{:S(2)}) collective-permute-start(bf16[3,4,64,256]{3,2,1,0:T(8,128)(2,1)S(1)} %get-tuple-element.200.refs_1_.refs_2_), channel_id=1, source_target_pairs={{0,8},{8,0},{16,24},{24,16},{1,9},{9,1},{17,25},{25,17},{2,10},{10... | collective-permute-start | bytes 1179656 | tf_op jit(solution)/shard_map/ppermute | solution.py:283
  84.7 14.0 %collective-permute-start.23 = (bf16[3,4,64,256]{3,2,1,0:T(8,128)(2,1)S(1)}, bf16[3,4,64,256]{3,2,1,0:T(8,128)(2,1)S(1)}, u32[]{:S(2)}, u32[]{:S(2)}) collective-permute-start(bf16[3,4,64,256]{3,2,1,0:T(8,128)(2,1)S(1)} %get-tuple-element.201.refs_0_.refs_1_), channel_id=1, source_target_pairs={{0,8},{8,0},{16,24},{24,16},{1,9},{9,1},{17,25},{25,17},{2,10},{10... | collective-permute-start | bytes 1179656 | tf_op jit(solution)/shard_map/ppermute | solution.py:283
  87.0 39.0 %collective-permute-start.31 = (bf16[3,3,4,64,256]{4,3,2,0,1:T(8,128)(2,1)}, bf16[3,3,4,64,256]{4,3,2,0,1:T(8,128)(2,1)S(1)}, u32[]{:S(2)}, u32[]{:S(2)}) collective-permute-start(bf16[3,3,4,64,256]{4,3,2,0,1:T(8,128)(2,1)} %get-tuple-element.186), channel_id=1, source_target_pairs={{0,16},{8,24},{16,0},{24,8},{1,17},{9,25},{17,1},{25,9},{2,18},{10... | collective-permute-start | bytes 3538952 | tf_op jit(solution)/shard_map/ppermute | solution.py:287
  90.0 19.9 %collective-permute-start.14 = (bf16[2,4,64,256]{3,2,1,0:T(8,128)(2,1)S(1)}, bf16[2,4,64,256]{3,2,1,0:T(8,128)(2,1)S(1)}, u32[]{:S(2)}, u32[]{:S(2)}) collective-permute-start(bf16[2,4,64,256]{3,2,1,0:T(8,128)(2,1)S(1)} %get-tuple-element.134), channel_id=1, source_target_pairs={{0,8},{8,0},{16,24},{24,16},{1,9},{9,1},{17,25},{25,17},{2,10},{10... | collective-permute-start | bytes 786440 | tf_op jit(solution)/shard_map/ppermute | solution.py:283
  98.6 11.4 %collective-permute-start.15 = (bf16[2,4,64,256]{3,2,1,0:T(8,128)(2,1)S(1)}, bf16[2,4,64,256]{3,2,1,0:T(8,128)(2,1)S(1)}, u32[]{:S(2)}, u32[]{:S(2)}) collective-permute-start(bf16[2,4,64,256]{3,2,1,0:T(8,128)(2,1)S(1)} %get-tuple-element.135), channel_id=1, source_target_pairs={{0,8},{8,0},{16,24},{24,16},{1,9},{9,1},{17,25},{25,17},{2,10},{10... | collective-permute-start | bytes 786440 | tf_op jit(solution)/shard_map/ppermute | solution.py:283
  99.0 11.0 %collective-permute-start.16 = (bf16[2,4,64,256]{3,2,1,0:T(8,128)(2,1)S(1)}, bf16[2,4,64,256]{3,2,1,0:T(8,128)(2,1)S(1)}, u32[]{:S(2)}, u32[]{:S(2)}) collective-permute-start(bf16[2,4,64,256]{3,2,1,0:T(8,128)(2,1)S(1)} %get-tuple-element.136), channel_id=1, source_target_pairs={{0,8},{8,0},{16,24},{24,16},{1,9},{9,1},{17,25},{25,17},{2,10},{10... | collective-permute-start | bytes 786440 | tf_op jit(solution)/shard_map/ppermute | solution.py:283
  110.4 31.9 %collective-permute-start.30 = (bf16[2,3,4,64,256]{4,3,2,0,1:T(8,128)(2,1)S(1)}, bf16[2,3,4,64,256]{4,3,2,0,1:T(8,128)(2,1)S(1)}, u32[]{:S(2)}, u32[]{:S(2)}) collective-permute-start(bf16[2,3,4,64,256]{4,3,2,0,1:T(8,128)(2,1)S(1)} %get-tuple-element.184), channel_id=1, source_target_pairs={{0,16},{8,24},{16,0},{24,8},{1,17},{9,25},{17,1},{25,9},{2,18},{10... | collective-permute-start | bytes 2359304 | tf_op jit(solution)/shard_map/ppermute | solution.py:287
  159.9 19.0 %collective-permute-start.38 = (bf16[4,32,2048]{2,1,0:T(8,128)(2,1)}, bf16[4,32,2048]{2,1,0:T(8,128)(2,1)}, u32[]{:S(2)}, u32[]{:S(2)}) collective-permute-start(bf16[4,32,2048]{2,1,0:T(8,128)(2,1)} %get-tuple-element.158.refs_11_), channel_id=1, source_target_pairs={{0,1},{1,0},{2,3},{3,2},{4,5},{5,4},{6,7},{7,6},{8,9},{9,8},{10,11... | collective-permute-start | bytes 1572872 | tf_op jit(solution)/shard_map/ppermute | solution.py:366
  160.5 19.8 %collective-permute-start.45 = (bf16[3,4,64,256]{3,2,1,0:T(8,128)(2,1)}, bf16[3,4,64,256]{3,2,1,0:T(8,128)(2,1)S(1)}, u32[]{:S(2)}, u32[]{:S(2)}) collective-permute-start(bf16[3,4,64,256]{3,2,1,0:T(8,128)(2,1)} %get-tuple-element.202.refs_0_), channel_id=1, source_target_pairs={{0,8},{8,0},{16,24},{24,16},{1,9},{9,1},{17,25},{25,17},{2,10},{10... | collective-permute-start | bytes 1179656 | tf_op jit(solution)/shard_map/ppermute | solution.py:283
  161.0 31.8 %collective-permute-start.43 = (bf16[3,4,64,256]{3,2,1,0:T(8,128)(2,1)}, bf16[3,4,64,256]{3,2,1,0:T(8,128)(2,1)S(1)}, u32[]{:S(2)}, u32[]{:S(2)}) collective-permute-start(bf16[3,4,64,256]{3,2,1,0:T(8,128)(2,1)} %get-tuple-element.196.refs_0_), channel_id=1, source_target_pairs={{0,8},{8,0},{16,24},{24,16},{1,9},{9,1},{17,25},{25,17},{2,10},{10... | collective-permute-start | bytes 1179656 | tf_op jit(solution)/shard_map/ppermute | solution.py:283
  161.0 33.2 %collective-permute-start.44 = (bf16[2,4,64,256]{3,2,1,0:T(8,128)(2,1)}, bf16[2,4,64,256]{3,2,1,0:T(8,128)(2,1)S(1)}, u32[]{:S(2)}, u32[]{:S(2)}) collective-permute-start(bf16[2,4,64,256]{3,2,1,0:T(8,128)(2,1)} %get-tuple-element.205.refs_6_), channel_id=1, source_target_pairs={{0,8},{8,0},{16,24},{24,16},{1,9},{9,1},{17,25},{25,17},{2,10},{10... | collective-permute-start | bytes 786440 | tf_op jit(solution)/shard_map/ppermute | solution.py:283
  163.1 25.9 %collective-permute-start.46 = (bf16[4,32,2048]{2,1,0:T(8,128)(2,1)}, bf16[4,32,2048]{2,1,0:T(8,128)(2,1)S(1)}, u32[]{:S(2)}, u32[]{:S(2)}) collective-permute-start(bf16[4,32,2048]{2,1,0:T(8,128)(2,1)} %copy-done.38), channel_id=1, source_target_pairs={{0,1},{1,0},{2,3},{3,2},{4,5},{5,4},{6,7},{7,6},{8,9},{9,8},{10,11... | collective-permute-start | bytes 1572872 | tf_op jit(solution)/shard_map/ppermute | solution.py:366
  189.5 21.0 %collective-permute-start.41 = (bf16[32,2048]{1,0:T(8,128)(2,1)S(1)}, bf16[32,2048]{1,0:T(8,128)(2,1)S(1)}, u32[]{:S(2)}, u32[]{:S(2)}) collective-permute-start(bf16[32,2048]{1,0:T(8,128)(2,1)S(1)} %get-tuple-element.212), channel_id=1, source_target_pairs={{0,4},{1,5},{2,6},{3,7},{4,0},{5,1},{6,2},{7,3},{8,12},{9,13},{10,... | collective-permute-start | bytes 393224 | tf_op jit(solution)/shard_map/ppermute | solution.py:342
  192.1 18.9 %collective-permute-start.42 = (bf16[32,2048]{1,0:T(8,128)(2,1)S(1)}, bf16[32,2048]{1,0:T(8,128)(2,1)S(1)}, u32[]{:S(2)}, u32[]{:S(2)}) collective-permute-start(bf16[32,2048]{1,0:T(8,128)(2,1)S(1)} %get-tuple-element.211), channel_id=1, source_target_pairs={{0,6},{1,7},{2,4},{3,5},{4,2},{5,3},{6,0},{7,1},{8,14},{9,15},{10,... | collective-permute-start | bytes 393224 | tf_op jit(solution)/shard_map/ppermute | solution.py:342
  192.8 18.3 %collective-permute-start.47 = (bf16[32,2048]{1,0:T(8,128)(2,1)S(1)}, bf16[32,2048]{1,0:T(8,128)(2,1)S(1)}, u32[]{:S(2)}, u32[]{:S(2)}) collective-permute-start(bf16[32,2048]{1,0:T(8,128)(2,1)S(1)} %get-tuple-element.216), channel_id=1, source_target_pairs={{0,2},{1,3},{2,0},{3,1},{4,6},{5,7},{6,4},{7,5},{8,10},{9,11},{10,... | collective-permute-start | bytes 393224 | tf_op jit(solution)/shard_map/ppermute | solution.py:342
  194.2 18.6 %collective-permute-start.48 = (bf16[32,2048]{1,0:T(8,128)(2,1)S(1)}, bf16[32,2048]{1,0:T(8,128)(2,1)S(1)}, u32[]{:S(2)}, u32[]{:S(2)}) collective-permute-start(bf16[32,2048]{1,0:T(8,128)(2,1)S(1)} %get-tuple-element.215), channel_id=1, source_target_pairs={{0,4},{1,5},{2,6},{3,7},{4,0},{5,1},{6,2},{7,3},{8,12},{9,13},{10,... | collective-permute-start | bytes 393224 | tf_op jit(solution)/shard_map/ppermute | solution.py:342
  196.4 18.8 %collective-permute-start.49 = (bf16[32,2048]{1,0:T(8,128)(2,1)S(1)}, bf16[32,2048]{1,0:T(8,128)(2,1)S(1)}, u32[]{:S(2)}, u32[]{:S(2)}) collective-permute-start(bf16[32,2048]{1,0:T(8,128)(2,1)S(1)} %get-tuple-element.214), channel_id=1, source_target_pairs={{0,6},{1,7},{2,4},{3,5},{4,2},{5,3},{6,0},{7,1},{8,14},{9,15},{10,... | collective-permute-start | bytes 393224 | tf_op jit(solution)/shard_map/ppermute | solution.py:342
  (59 other events, 325.0 us)

commit v3 on v2

--- a/solution.py
+++ b/solution.py
@@ -269,7 +269,7 @@
     sizes = [1, 2, 3, 3, 3, 2]
     pieces = [(0, 0, 1), (1, 0, 2), (2, 0, 3), (3, 0, 3), (4, 0, 3), (5, 0, 2)]
     steps = (
-        "F0", "S0", "F1", "S1", "F2", "F3", "L0", "S2", "F4", "L1", "S3", "F5", "I0,1", "L2", "S4", "W0,1",
+        "F0", "S0", "F1", "S1", "F2", "L0", "S2", "F3", "F4", "L1", "S3", "F5", "I0,1", "L2", "S4", "W0,1",
         "I2", "L3", "S5", "I3", "L4", "I4", "L5", "E5", "W2", "X0", "W3", "X1", "W4,5",
     )
     return sizes, pieces, steps, 2

time: 221 us -> 221 us (level)
  local copies, waits for them, and re-layouts: 21.5 us -> 18.9 us
    add x6, other arithmetic: 3.02 us -> 5.61 us  [shards(): total = total + other.astype(F32)]
    convert_element_type x5, local copies, waits for them, and re-layouts: 4.37 us -> 1.8 us  [shards(): sent = mine[what].astype(BF16)]
  transfers between devices with their start and end apart: 50 -> 50, of which waited for: 17 -> 21; matrix products, arithmetic and copies ran while one was open for 9% -> 8% of each run, Pallas kernels for 51% -> 51%
where the time goes in v3:
time: 221 us; the launch traced here: 217 us
  Pallas kernels  130 us (59%)
  starting transfers between devices  24.3 us (11%)
  waiting for transfers between devices  23 us (10%)
  local copies, waits for them, and re-layouts  18.9 us (9%)
  other arithmetic  18.6 us (8%)
    pallas_call x9, Pallas kernels, backward(): pl.pallas_call(kernel, grid_spec=pltpu.PrefetchScalarGridSpec(num_scalar_...  82.3 us
    pallas_call x6, Pallas kernels, forward(): pl.pallas_call(kernel, grid_spec=pltpu.PrefetchScalarGridSpec(num_scalar_...  47.8 us
    unnamed x83, local copies, waits for them, and re-layouts  17 us
    ppermute x36, waiting for transfers between devices, swap_core(): return lax.ppermute(v, 'row', [(i, i ^ 1) for i in range(n_row)])  10.4 us
    ppermute x36, starting transfers between devices, swap_core(): return lax.ppermute(v, 'row', [(i, i ^ 1) for i in range(n_row)])  9.17 us
    ppermute x6, waiting for transfers between devices, from_y(): lax.ppermute(v, 'row', [(i, (i + 2 * s) % n_row) for i in range(n_row)])  7.83 us
    ppermute x6, starting transfers between devices, shards(): lax.ppermute(out, 'col', [(j, j ^ 2 * s) for j in range(n_col)])  7.83 us
    add x6, other arithmetic, shards(): total = total + other.astype(F32)  5.61 us
  transfers between devices with their start and end apart: 50, of which 21 were waited for; matrix products, arithmetic and copies ran while one was open for 8% of the time, Pallas kernels for 51%

profile of v3, /device:TPU:14, one launch (start us, length us, event | category | flops | bytes accessed | tf_op | source)
XLA Modules:
  0.0 216.5 jit_solution(6453636853204366237)
XLA Ops:
  1.4 1.6 copy-done.10
  3.0 1.6 copy-done.11
  6.0 5.1 %forward_t1.1 = (f32[1,3,4,64,256]{4,3,2,1,0:T(8,128)S(1)}, bf16[1,4,64,256]{3,2,1,0:T(8,128)(2,1)S(1)}, bf16[1,4,64,256]{3,2,1,0:T(8,128)(2,1)S(1)}, bf16[1,4,6...) custom-call(s32[1]{0:T(128)} %bitcast.1.core_ref, ...), custom_call_target="tpu_custom_call" | custom-call | flops 8400000 | tf_op jit(solution)/shard_map/forward_t1/pallas_call | solution.py:84
  13.2 7.4 %forward_t2.2 = (f32[2,3,4,64,256]{4,3,2,1,0:T(8,128)S(1)}, bf16[2,4,64,256]{3,2,1,0:T(8,128)(2,1)S(1)}, bf16[2,4,64,256]{3,2,1,0:T(8,128)(2,1)S(1)}, bf16[2,4,64,256]{3,2,1,0:T(8,128)(2,1)S(1)}) custom-call(s32[1]{0:T(128)} %bitcast.1.core_ref, s32[16,28]{1,0:T(8,128)S(1)} %copy-done.12, s32[16,28]{1,0:T(8,128)S(1)} %copy-done.16, s32[28,16]{1,0:T(8,128)S(1)} %copy.42.dm, ...), custom_call_target="tpu_custom_call" | custom-call | flops 16800000 | tf_op jit(solution)/shard_map/forward_t2/pallas_call | solution.py:84
  23.9 9.3 %forward_t3.3 = (f32[3,3,4,64,256]{4,3,2,1,0:T(8,128)S(1)}, bf16[3,4,64,256]{3,2,1,0:T(8,128)(2,1)S(1)}, bf16[3,4,64,256]{3,2,1,0:T(8,128)(2,1)S(1)}, bf16[3,4,64,256]{3,2,1,0:T(8,128)(2,1)S(1)}) custom-call(s32[1]{0:T(128)} %bitcast.1.core_ref, s32[16,28]{1,0:T(8,128)S(1)} %copy-done.12, s32[16,28]{1,0:T(8,128)S(1)} %copy-done.16, s32[28,16]{1,0:T(8,128)S(1)} %copy.42.dm, ...), custom_call_target="tpu_custom_call" | custom-call | flops 25200000 | tf_op jit(solution)/shard_map/forward_t3/pallas_call | solution.py:84
  36.5 1.6 collective-permute-start.18
  38.3 9.4 %forward_t3.4 = (f32[3,3,4,64,256]{4,3,2,1,0:T(8,128)S(1)}, bf16[3,4,64,256]{3,2,1,0:T(8,128)(2,1)S(1)}, bf16[3,4,64,256]{3,2,1,0:T(8,128)(2,1)S(1)}, bf16[3,4,64,256]{3,2,1,0:T(8,128)(2,1)S(1)}) custom-call(s32[1]{0:T(128)} %bitcast.1.core_ref, s32[16,28]{1,0:T(8,128)S(1)} %copy-done.12, s32[16,28]{1,0:T(8,128)S(1)} %copy-done.16, s32[28,16]{1,0:T(8,128)S(1)} %copy.42.dm, ...), custom_call_target="tpu_custom_call" | custom-call | flops 25200000 | tf_op jit(solution)/shard_map/forward_t3/pallas_call | solution.py:84
  48.3 9.3 %forward_t3.5 = (f32[3,3,4,64,256]{4,3,2,1,0:T(8,128)S(1)}, bf16[3,4,64,256]{3,2,1,0:T(8,128)(2,1)S(1)}, bf16[3,4,64,256]{3,2,1,0:T(8,128)(2,1)S(1)}, bf16[3,4,64,256]{3,2,1,0:T(8,128)(2,1)S(1)}) custom-call(s32[1]{0:T(128)} %bitcast.1.core_ref, s32[16,28]{1,0:T(8,128)S(1)} %copy-done.12, s32[16,28]{1,0:T(8,128)S(1)} %copy-done.16, s32[28,16]{1,0:T(8,128)S(1)} %copy.42.dm, ...), custom_call_target="tpu_custom_call" | custom-call | flops 25200000 | tf_op jit(solution)/shard_map/forward_t3/pallas_call | solution.py:84
  59.9 1.9 fusion.14
  62.4 7.2 %forward_t2.3 = (f32[2,3,4,64,256]{4,3,2,1,0:T(8,128)S(1)}, bf16[2,4,64,256]{3,2,1,0:T(8,128)(2,1)S(1)}, bf16[2,4,64,256]{3,2,1,0:T(8,128)(2,1)S(1)}, bf16[2,4,64,256]{3,2,1,0:T(8,128)(2,1)S(1)}) custom-call(s32[1]{0:T(128)} %bitcast.1.core_ref, s32[16,28]{1,0:T(8,128)S(1)} %copy-done.12, s32[16,28]{1,0:T(8,128)S(1)} %copy-done.16, s32[28,16]{1,0:T(8,128)S(1)} %copy.42.dm, ...), custom_call_target="tpu_custom_call" | custom-call | flops 16800000 | tf_op jit(solution)/shard_map/forward_t2/pallas_call | solution.py:84
  70.3 8.8 %backward_input_t3.4.refs_6_ = f32[512,2048]{1,0:T(8,128)S(1)} custom-call(s32[1]{0:T(128)} %constant.60.clone.1.xi, s32[16,28]{1,0:T(8,128)S(1)} %copy-done.13, s32[16,28]{1,0:T(8,128)S(1)} %copy-done.16, s32[28,16]{1,0:T(8,128)S(1)} %copy.42.dm, bf16[1,4,64,256]{3,2,1,0:T(8,128)(2,1)S(1)} %get-tuple-element.218.refs_0_.refs_1_, ...), custom_call_target="tpu_custom_call" | custom-call | flops 25200000 | tf_op jit(solution)/shard_map/backward_input_t3/pallas_call | solution.py:229
  79.7 1.6 convert_add_fusion.2
  83.1 2.3 %fusion.13 = (bf16[3,3,4,64,256]{4,3,2,0,1:T(8,128)(2,1)}, f32[3,3,4,64,256]{4,3,2,0,1:T(8,128)}) fusion(bf16[3,1,4,64,256]{4,3,2,0,1:T(8,128)(2,1)S(1)} %bitcast.172, bf16[3,1,4,64,256]{4,3,2,0,1:T(8,128)(2,1)S(1)} %bitcast.171, bf16[3,1,4,64,256]{4,3,2,0,1:T(8,128)(2,1)S(1)} %bitcast.169, f32[3,3,4,64,256]{4,3,2,1,0:T(8,128)S(1)} %get-tuple-element.142), kind=kLoop, calls=%fused_computation.80 | loop fusion | flops 2949120 | bytes 7077888 | tf_op jit(solution)/shard_map/convert_element_type | solution.py:325
  88.7 8.4 %backward_weight_t3.3 = (bf16[2048,3584]{1,0:T(8,128)(2,1)}, bf16[2048,3584]{1,0:T(8,128)(2,1)}, bf16[3584,2048]{1,0:T(8,128)(2,1)}) custom-call(s32[1]{0:T(128)} %constant.60.clone.1.xi, s32[16,28]{1,0:T(8,128)S(1)} %copy-done.13, s32[16,28]{1,0:T(8,128)S(1)} %copy-done.16, s32[28,16]{1,0:T(8,128)S(1)} %copy.42.dm, ...), custom_call_target="tpu_custom_call" | custom-call | flops 25200000 | tf_op jit(solution)/shard_map/backward_weight_t3/pallas_call | solution.py:229
  97.6 8.6 %backward_input_t3.5.refs_6_ = f32[512,2048]{1,0:T(8,128)S(1)} custom-call(s32[1]{0:T(128)} %constant.60.clone.1.xi, s32[16,28]{1,0:T(8,128)S(1)} %copy-done.13, s32[16,28]{1,0:T(8,128)S(1)} %copy-done.16, s32[28,16]{1,0:T(8,128)S(1)} %copy.42.dm, bf16[3,4,64,256]{3,2,1,0:T(8,128)(2,1)S(1)} %get-tuple-element.201.refs_0_.refs_1_, ...), custom_call_target="tpu_custom_call" | custom-call | flops 25200000 | tf_op jit(solution)/shard_map/backward_input_t3/pallas_call | solution.py:229
  106.3 1.7 convert_add_fusion.1
  111.6 8.6 %backward_input_t3.6.refs_6_ = f32[512,2048]{1,0:T(8,128)S(1)} custom-call(s32[1]{0:T(128)} %constant.60.clone.1.xi, s32[16,28]{1,0:T(8,128)S(1)} %copy-done.13, s32[16,28]{1,0:T(8,128)S(1)} %copy-done.16, s32[28,16]{1,0:T(8,128)S(1)} %copy.42.dm, bf16[3,4,64,256]{3,2,1,0:T(8,128)(2,1)S(1)} %get-tuple-element.203.refs_0_.refs_1_, ...), custom_call_target="tpu_custom_call" | custom-call | flops 25200000 | tf_op jit(solution)/shard_map/backward_input_t3/pallas_call | solution.py:229
  120.2 5.9 %collective-permute-done.31 = bf16[3,3,4,64,256]{4,3,2,0,1:T(8,128)(2,1)} collective-permute-done((bf16[3,3,4,64,256]{4,3,2,0,1:T(8,128)(2,1)}, bf16[3,3,4,64,256]{4,3,2,0,1:T(8,128)(2,1)}, u32[]{:S(2)}, u32[]{:S(2)}) %collective-permute-start.31) | collective-permute-done | bytes 1179680 | tf_op jit(solution)/shard_map/ppermute | solution.py:287
  126.1 1.7 convert_add_fusion
  131.4 8.9 %backward_input_t3.7.refs_6_ = f32[512,2048]{1,0:T(8,128)S(1)} custom-call(s32[1]{0:T(128)} %constant.60.clone.1.xi, s32[16,28]{1,0:T(8,128)S(1)} %copy-done.13, s32[16,28]{1,0:T(8,128)S(1)} %copy-done.16, s32[28,16]{1,0:T(8,128)S(1)} %copy.42.dm, bf16[3,4,64,256]{3,2,1,0:T(8,128)(2,1)S(1)} %get-tuple-element.198.refs_0_.refs_1_, ...), custom_call_target="tpu_custom_call" | custom-call | flops 25200000 | tf_op jit(solution)/shard_map/backward_input_t3/pallas_call | solution.py:229
  140.3 1.9 collective-permute-done.30
  144.1 1.7 collective-permute-done.36.refs_2_.refs_10_
  145.8 2.2 %copy-done.3 = f32[512,2048]{1,0:T(8,128)S(1)} copy-done((f32[512,2048]{1,0:T(8,128)S(1)}, f32[512,2048]{1,0:T(8,128)}, u32[]{:S(2)}) %copy-start.3) | copy-done | bytes 4194328
  149.4 7.8 %backward_input_t2.1 = (bf16[4,32,2048]{2,1,0:T(8,128)(2,1)}, bf16[4,32,2048]{2,1,0:T(8,128)(2,1)S(1)}, f32[4,32,2048]{2,1,0:T(8,128)S(1)}, f32[4,32,2048]{2,1,0:T(8,128)S(1)}) custom-call(s32[1]{0:T(128)} %bitcast.xi, s32[16,28]{1,0:T(8,128)S(1)} %copy-done.14, s32[16,28]{1,0:T(8,128)S(1)} %copy-done.17, s32[28,16]{1,0:T(8,128)S(1)} %copy.42.dm, ...), custom_call_target="tpu_custom_call" | custom-call | flops 16800000 | tf_op jit(solution)/shard_map/backward_input_t2/pallas_call | solution.py:229
  164.5 1.6 copy-done.1
  169.5 9.3 %backward_weight_t3.4 = (bf16[2048,3584]{1,0:T(8,128)(2,1)}, bf16[2048,3584]{1,0:T(8,128)(2,1)}, bf16[3584,2048]{1,0:T(8,128)(2,1)}) custom-call(s32[1]{0:T(128)} %constant.60.clone.1.xi, s32[16,28]{1,0:T(8,128)S(1)} %copy-done.15, s32[16,28]{1,0:T(8,128)S(1)} %copy-done.18, ...), custom_call_target="tpu_custom_call", output_to_operand_aliasing={{0}: (12, {}), {1}: (13, {}), {2}: (14, {})} | custom-call | flops 25200000 | tf_op jit(solution)/shard_map/backward_weight_t3/pallas_call | solution.py:229
  180.5 8.4 %backward_weight_t3.5 = (bf16[2048,3584]{1,0:T(8,128)(2,1)}, bf16[2048,3584]{1,0:T(8,128)(2,1)}, bf16[3584,2048]{1,0:T(8,128)(2,1)}) custom-call(s32[1]{0:T(128)} %constant.60.clone.1.xi, s32[16,28]{1,0:T(8,128)S(1)} %copy-done.15, s32[16,28]{1,0:T(8,128)S(1)} %copy-done.18, ...), custom_call_target="tpu_custom_call", output_to_operand_aliasing={{0}: (12, {}), {1}: (13, {}), {2}: (14, {})} | custom-call | flops 25200000 | tf_op jit(solution)/shard_map/backward_weight_t3/pallas_call | solution.py:229
  189.5 2.6 %collective-permute-start.41 = (bf16[32,2048]{1,0:T(8,128)(2,1)S(1)}, bf16[32,2048]{1,0:T(8,128)(2,1)S(1)}, u32[]{:S(2)}, u32[]{:S(2)}) collective-permute-start(bf16[32,2048]{1,0:T(8,128)(2,1)S(1)} %get-tuple-element.212), channel_id=1, source_target_pairs={{0,4},{1,5},{2,6},{3,7},{4,0},{5,1},{6,2},{7,3},{8,12},{9,13},{10,... | collective-permute-start | bytes 393224 | tf_op jit(solution)/shard_map/ppermute | solution.py:342
  194.2 2.2 %collective-permute-start.48 = (bf16[32,2048]{1,0:T(8,128)(2,1)S(1)}, bf16[32,2048]{1,0:T(8,128)(2,1)S(1)}, u32[]{:S(2)}, u32[]{:S(2)}) collective-permute-start(bf16[32,2048]{1,0:T(8,128)(2,1)S(1)} %get-tuple-element.215), channel_id=1, source_target_pairs={{0,4},{1,5},{2,6},{3,7},{4,0},{5,1},{6,2},{7,3},{8,12},{9,13},{10,... | collective-permute-start | bytes 393224 | tf_op jit(solution)/shard_map/ppermute | solution.py:342
  197.1 13.4 %backward_weight_t5.1 = (bf16[2048,3584]{1,0:T(8,128)(2,1)}, bf16[2048,3584]{1,0:T(8,128)(2,1)}, bf16[3584,2048]{1,0:T(8,128)(2,1)}) custom-call(s32[1]{0:T(128)} %constant.60.clone.1.xi, s32[16,28]{1,0:T(8,128)S(1)} %copy-done.15, s32[16,28]{1,0:T(8,128)S(1)} %copy-done.18, ...), custom_call_target="tpu_custom_call", output_to_operand_aliasing={{0}: (18, {}), {1}: (19, {}), {2}: (20, {})} | custom-call | flops 42000000 | tf_op jit(solution)/shard_map/backward_weight_t5/pallas_call | solution.py:229
  211.0 1.8 collective-permute-done.48
  212.8 2.5 %collective-permute-done.49 = bf16[32,2048]{1,0:T(8,128)(2,1)S(1)} collective-permute-done((bf16[32,2048]{1,0:T(8,128)(2,1)S(1)}, bf16[32,2048]{1,0:T(8,128)(2,1)S(1)}, u32[]{:S(2)}, u32[]{:S(2)}) %collective-permute-start.49) | collective-permute-done | bytes 131104 | tf_op jit(solution)/shard_map/ppermute | solution.py:342
  (197 shorter events, 48.4 us)
Async XLA Ops:
  21.3 12.6 %collective-permute-start.9 = (bf16[1,3,4,64,256]{4,3,2,1,0:T(8,128)(2,1)S(1)}, bf16[1,3,4,64,256]{4,3,2,1,0:T(8,128)(2,1)S(1)}, u32[]{:S(2)}, u32[]{:S(2)}) collective-permute-start(bf16[1,3,4,64,256]{4,3,2,1,0:T(8,128)(2,1)S(1)} %get-tuple-element.194.rest_0_), channel_id=1, source_target_pairs={{0,16},{8,24},{16,0},{24,8},{1,17},{9,25},{17,1},{25,9},{2,18},{10... | collective-permute-start | bytes 1179656 | tf_op jit(solution)/shard_map/ppermute | solution.py:287
  23.3 34.3 %collective-permute-start.13 = (bf16[2,3,4,64,256]{4,3,2,0,1:T(8,128)(2,1)S(1)}, bf16[2,3,4,64,256]{4,3,2,0,1:T(8,128)(2,1)S(1)}, u32[]{:S(2)}, u32[]{:S(2)}) collective-permute-start(bf16[2,3,4,64,256]{4,3,2,0,1:T(8,128)(2,1)S(1)} %get-tuple-element.192), channel_id=1, source_target_pairs={{0,16},{8,24},{16,0},{24,8},{1,17},{9,25},{17,1},{25,9},{2,18},{10... | collective-permute-start | bytes 2359304 | tf_op jit(solution)/shard_map/ppermute | solution.py:287
  36.5 42.6 %collective-permute-start.18 = (bf16[3,3,4,64,256]{4,3,2,0,1:T(8,128)(2,1)S(1)}, bf16[3,3,4,64,256]{4,3,2,0,1:T(8,128)(2,1)}, u32[]{:S(2)}, u32[]{:S(2)}) collective-permute-start(bf16[3,3,4,64,256]{4,3,2,0,1:T(8,128)(2,1)S(1)} %get-tuple-element.190), channel_id=1, source_target_pairs={{0,16},{8,24},{16,0},{24,8},{1,17},{9,25},{17,1},{25,9},{2,18},{10... | collective-permute-start | bytes 3538952 | tf_op jit(solution)/shard_map/ppermute | solution.py:287
  38.1 31.5 %collective-permute-start.20 = (bf16[1,4,64,256]{3,2,1,0:T(8,128)(2,1)S(1)}, bf16[1,4,64,256]{3,2,1,0:T(8,128)(2,1)S(1)}, u32[]{:S(2)}, u32[]{:S(2)}) collective-permute-start(bf16[1,4,64,256]{3,2,1,0:T(8,128)(2,1)S(1)} %get-tuple-element.219.refs_1_.refs_2_), channel_id=1, source_target_pairs={{0,8},{8,0},{16,24},{24,16},{1,9},{9,1},{17,25},{25,17},{2,10},{10... | collective-permute-start | bytes 393224 | tf_op jit(solution)/shard_map/ppermute | solution.py:283
  47.6 11.1 %collective-permute-start.10 = (bf16[3,4,64,256]{3,2,1,0:T(8,128)(2,1)S(1)}, bf16[3,4,64,256]{3,2,1,0:T(8,128)(2,1)S(1)}, u32[]{:S(2)}, u32[]{:S(2)}) collective-permute-start(bf16[3,4,64,256]{3,2,1,0:T(8,128)(2,1)S(1)} %get-tuple-element.123), channel_id=1, source_target_pairs={{0,8},{8,0},{16,24},{24,16},{1,9},{9,1},{17,25},{25,17},{2,10},{10... | collective-permute-start | bytes 1179656 | tf_op jit(solution)/shard_map/ppermute | solution.py:283
  48.2 10.7 %collective-permute-start.11 = (bf16[3,4,64,256]{3,2,1,0:T(8,128)(2,1)S(1)}, bf16[3,4,64,256]{3,2,1,0:T(8,128)(2,1)S(1)}, u32[]{:S(2)}, u32[]{:S(2)}) collective-permute-start(bf16[3,4,64,256]{3,2,1,0:T(8,128)(2,1)S(1)} %get-tuple-element.124), channel_id=1, source_target_pairs={{0,8},{8,0},{16,24},{24,16},{1,9},{9,1},{17,25},{25,17},{2,10},{10... | collective-permute-start | bytes 1179656 | tf_op jit(solution)/shard_map/ppermute | solution.py:283
  58.9 11.4 %collective-permute-start.22 = (bf16[2,4,64,256]{3,2,1,0:T(8,128)(2,1)S(1)}, bf16[2,4,64,256]{3,2,1,0:T(8,128)(2,1)S(1)}, u32[]{:S(2)}, u32[]{:S(2)}) collective-permute-start(bf16[2,4,64,256]{3,2,1,0:T(8,128)(2,1)S(1)} %get-tuple-element.210.refs_5_.refs_8_), channel_id=1, source_target_pairs={{0,8},{8,0},{16,24},{24,16},{1,9},{9,1},{17,25},{25,17},{2,10},{10... | collective-permute-start | bytes 786440 | tf_op jit(solution)/shard_map/ppermute | solution.py:283
  59.5 10.2 %collective-permute-start.21 = (bf16[2,4,64,256]{3,2,1,0:T(8,128)(2,1)S(1)}, bf16[2,4,64,256]{3,2,1,0:T(8,128)(2,1)S(1)}, u32[]{:S(2)}, u32[]{:S(2)}) collective-permute-start(bf16[2,4,64,256]{3,2,1,0:T(8,128)(2,1)S(1)} %get-tuple-element.209.refs_4_.refs_7_), channel_id=1, source_target_pairs={{0,8},{8,0},{16,24},{24,16},{1,9},{9,1},{17,25},{25,17},{2,10},{10... | collective-permute-start | bytes 786440 | tf_op jit(solution)/shard_map/ppermute | solution.py:283
  61.7 44.5 %collective-permute-start.17 = (bf16[3,3,4,64,256]{4,3,2,0,1:T(8,128)(2,1)S(1)}, bf16[3,3,4,64,256]{4,3,2,0,1:T(8,128)(2,1)}, u32[]{:S(2)}, u32[]{:S(2)}) collective-permute-start(bf16[3,3,4,64,256]{4,3,2,0,1:T(8,128)(2,1)S(1)} %get-tuple-element.188), channel_id=1, source_target_pairs={{0,16},{8,24},{16,0},{24,8},{1,17},{9,25},{17,1},{25,9},{2,18},{10... | collective-permute-start | bytes 3538952 | tf_op jit(solution)/shard_map/ppermute | solution.py:287
  69.6 15.9 %collective-permute-start.25 = (bf16[1,4,64,256]{3,2,1,0:T(8,128)(2,1)S(1)}, bf16[1,4,64,256]{3,2,1,0:T(8,128)(2,1)S(1)}, u32[]{:S(2)}, u32[]{:S(2)}) collective-permute-start(bf16[1,4,64,256]{3,2,1,0:T(8,128)(2,1)S(1)} %get-tuple-element.217.refs_0_), channel_id=1, source_target_pairs={{0,8},{8,0},{16,24},{24,16},{1,9},{9,1},{17,25},{25,17},{2,10},{10... | collective-permute-start | bytes 393224 | tf_op jit(solution)/shard_map/ppermute | solution.py:283
  69.7 12.8 %collective-permute-start.27 = (bf16[3,4,64,256]{3,2,1,0:T(8,128)(2,1)S(1)}, bf16[3,4,64,256]{3,2,1,0:T(8,128)(2,1)S(1)}, u32[]{:S(2)}, u32[]{:S(2)}) collective-permute-start(bf16[3,4,64,256]{3,2,1,0:T(8,128)(2,1)S(1)} %get-tuple-element.139), channel_id=1, source_target_pairs={{0,8},{8,0},{16,24},{24,16},{1,9},{9,1},{17,25},{25,17},{2,10},{10... | collective-permute-start | bytes 1179656 | tf_op jit(solution)/shard_map/ppermute | solution.py:283
  70.2 12.4 %collective-permute-start.28 = (bf16[3,4,64,256]{3,2,1,0:T(8,128)(2,1)S(1)}, bf16[3,4,64,256]{3,2,1,0:T(8,128)(2,1)S(1)}, u32[]{:S(2)}, u32[]{:S(2)}) collective-permute-start(bf16[3,4,64,256]{3,2,1,0:T(8,128)(2,1)S(1)} %get-tuple-element.140), channel_id=1, source_target_pairs={{0,8},{8,0},{16,24},{24,16},{1,9},{9,1},{17,25},{25,17},{2,10},{10... | collective-permute-start | bytes 1179656 | tf_op jit(solution)/shard_map/ppermute | solution.py:283
  79.2 3.9 %collective-permute-start.29 = (bf16[3,4,64,256]{3,2,1,0:T(8,128)(2,1)S(1)}, bf16[3,4,64,256]{3,2,1,0:T(8,128)(2,1)S(1)}, u32[]{:S(2)}, u32[]{:S(2)}) collective-permute-start(bf16[3,4,64,256]{3,2,1,0:T(8,128)(2,1)S(1)} %get-tuple-element.141), channel_id=1, source_target_pairs={{0,8},{8,0},{16,24},{24,16},{1,9},{9,1},{17,25},{25,17},{2,10},{10... | collective-permute-start | bytes 1179656 | tf_op jit(solution)/shard_map/ppermute | solution.py:283
  82.6 5.9 %collective-permute-start.26 = (bf16[2,4,64,256]{3,2,1,0:T(8,128)(2,1)S(1)}, bf16[2,4,64,256]{3,2,1,0:T(8,128)(2,1)S(1)}, u32[]{:S(2)}, u32[]{:S(2)}) collective-permute-start(bf16[2,4,64,256]{3,2,1,0:T(8,128)(2,1)S(1)} %get-tuple-element.208.refs_6_), channel_id=1, source_target_pairs={{0,8},{8,0},{16,24},{24,16},{1,9},{9,1},{17,25},{25,17},{2,10},{10... | collective-permute-start | bytes 786440 | tf_op jit(solution)/shard_map/ppermute | solution.py:283
  82.6 14.8 %collective-permute-start.24 = (bf16[3,4,64,256]{3,2,1,0:T(8,128)(2,1)S(1)}, bf16[3,4,64,256]{3,2,1,0:T(8,128)(2,1)S(1)}, u32[]{:S(2)}, u32[]{:S(2)}) collective-permute-start(bf16[3,4,64,256]{3,2,1,0:T(8,128)(2,1)S(1)} %get-tuple-element.200.refs_1_.refs_2_), channel_id=1, source_target_pairs={{0,8},{8,0},{16,24},{24,16},{1,9},{9,1},{17,25},{25,17},{2,10},{10... | collective-permute-start | bytes 1179656 | tf_op jit(solution)/shard_map/ppermute | solution.py:283
  83.1 14.0 %collective-permute-start.23 = (bf16[3,4,64,256]{3,2,1,0:T(8,128)(2,1)S(1)}, bf16[3,4,64,256]{3,2,1,0:T(8,128)(2,1)S(1)}, u32[]{:S(2)}, u32[]{:S(2)}) collective-permute-start(bf16[3,4,64,256]{3,2,1,0:T(8,128)(2,1)S(1)} %get-tuple-element.201.refs_0_.refs_1_), channel_id=1, source_target_pairs={{0,8},{8,0},{16,24},{24,16},{1,9},{9,1},{17,25},{25,17},{2,10},{10... | collective-permute-start | bytes 1179656 | tf_op jit(solution)/shard_map/ppermute | solution.py:283
  85.5 40.6 %collective-permute-start.31 = (bf16[3,3,4,64,256]{4,3,2,0,1:T(8,128)(2,1)}, bf16[3,3,4,64,256]{4,3,2,0,1:T(8,128)(2,1)}, u32[]{:S(2)}, u32[]{:S(2)}) collective-permute-start(bf16[3,3,4,64,256]{4,3,2,0,1:T(8,128)(2,1)} %get-tuple-element.186), channel_id=1, source_target_pairs={{0,16},{8,24},{16,0},{24,8},{1,17},{9,25},{17,1},{25,9},{2,18},{10... | collective-permute-start | bytes 3538952 | tf_op jit(solution)/shard_map/ppermute | solution.py:287
  88.5 21.2 %collective-permute-start.14 = (bf16[2,4,64,256]{3,2,1,0:T(8,128)(2,1)S(1)}, bf16[2,4,64,256]{3,2,1,0:T(8,128)(2,1)S(1)}, u32[]{:S(2)}, u32[]{:S(2)}) collective-permute-start(bf16[2,4,64,256]{3,2,1,0:T(8,128)(2,1)S(1)} %get-tuple-element.134), channel_id=1, source_target_pairs={{0,8},{8,0},{16,24},{24,16},{1,9},{9,1},{17,25},{25,17},{2,10},{10... | collective-permute-start | bytes 786440 | tf_op jit(solution)/shard_map/ppermute | solution.py:283
  97.1 12.7 %collective-permute-start.15 = (bf16[2,4,64,256]{3,2,1,0:T(8,128)(2,1)S(1)}, bf16[2,4,64,256]{3,2,1,0:T(8,128)(2,1)S(1)}, u32[]{:S(2)}, u32[]{:S(2)}) collective-permute-start(bf16[2,4,64,256]{3,2,1,0:T(8,128)(2,1)S(1)} %get-tuple-element.135), channel_id=1, source_target_pairs={{0,8},{8,0},{16,24},{24,16},{1,9},{9,1},{17,25},{25,17},{2,10},{10... | collective-permute-start | bytes 786440 | tf_op jit(solution)/shard_map/ppermute | solution.py:283
  97.5 12.3 %collective-permute-start.16 = (bf16[2,4,64,256]{3,2,1,0:T(8,128)(2,1)S(1)}, bf16[2,4,64,256]{3,2,1,0:T(8,128)(2,1)S(1)}, u32[]{:S(2)}, u32[]{:S(2)}) collective-permute-start(bf16[2,4,64,256]{3,2,1,0:T(8,128)(2,1)S(1)} %get-tuple-element.136), channel_id=1, source_target_pairs={{0,8},{8,0},{16,24},{24,16},{1,9},{9,1},{17,25},{25,17},{2,10},{10... | collective-permute-start | bytes 786440 | tf_op jit(solution)/shard_map/ppermute | solution.py:283
  110.2 32.1 %collective-permute-start.30 = (bf16[2,3,4,64,256]{4,3,2,0,1:T(8,128)(2,1)S(1)}, bf16[2,3,4,64,256]{4,3,2,0,1:T(8,128)(2,1)S(1)}, u32[]{:S(2)}, u32[]{:S(2)}) collective-permute-start(bf16[2,3,4,64,256]{4,3,2,0,1:T(8,128)(2,1)S(1)} %get-tuple-element.184), channel_id=1, source_target_pairs={{0,16},{8,24},{16,0},{24,8},{1,17},{9,25},{17,1},{25,9},{2,18},{10... | collective-permute-start | bytes 2359304 | tf_op jit(solution)/shard_map/ppermute | solution.py:287
  159.9 19.0 %collective-permute-start.38 = (bf16[4,32,2048]{2,1,0:T(8,128)(2,1)}, bf16[4,32,2048]{2,1,0:T(8,128)(2,1)}, u32[]{:S(2)}, u32[]{:S(2)}) collective-permute-start(bf16[4,32,2048]{2,1,0:T(8,128)(2,1)} %get-tuple-element.158.refs_11_), channel_id=1, source_target_pairs={{0,1},{1,0},{2,3},{3,2},{4,5},{5,4},{6,7},{7,6},{8,9},{9,8},{10,11... | collective-permute-start | bytes 1572872 | tf_op jit(solution)/shard_map/ppermute | solution.py:366
  160.5 19.8 %collective-permute-start.45 = (bf16[3,4,64,256]{3,2,1,0:T(8,128)(2,1)}, bf16[3,4,64,256]{3,2,1,0:T(8,128)(2,1)S(1)}, u32[]{:S(2)}, u32[]{:S(2)}) collective-permute-start(bf16[3,4,64,256]{3,2,1,0:T(8,128)(2,1)} %get-tuple-element.202.refs_0_), channel_id=1, source_target_pairs={{0,8},{8,0},{16,24},{24,16},{1,9},{9,1},{17,25},{25,17},{2,10},{10... | collective-permute-start | bytes 1179656 | tf_op jit(solution)/shard_map/ppermute | solution.py:283
  161.0 31.8 %collective-permute-start.43 = (bf16[3,4,64,256]{3,2,1,0:T(8,128)(2,1)}, bf16[3,4,64,256]{3,2,1,0:T(8,128)(2,1)S(1)}, u32[]{:S(2)}, u32[]{:S(2)}) collective-permute-start(bf16[3,4,64,256]{3,2,1,0:T(8,128)(2,1)} %get-tuple-element.196.refs_0_), channel_id=1, source_target_pairs={{0,8},{8,0},{16,24},{24,16},{1,9},{9,1},{17,25},{25,17},{2,10},{10... | collective-permute-start | bytes 1179656 | tf_op jit(solution)/shard_map/ppermute | solution.py:283
  161.0 33.2 %collective-permute-start.44 = (bf16[2,4,64,256]{3,2,1,0:T(8,128)(2,1)}, bf16[2,4,64,256]{3,2,1,0:T(8,128)(2,1)S(1)}, u32[]{:S(2)}, u32[]{:S(2)}) collective-permute-start(bf16[2,4,64,256]{3,2,1,0:T(8,128)(2,1)} %get-tuple-element.205.refs_6_), channel_id=1, source_target_pairs={{0,8},{8,0},{16,24},{24,16},{1,9},{9,1},{17,25},{25,17},{2,10},{10... | collective-permute-start | bytes 786440 | tf_op jit(solution)/shard_map/ppermute | solution.py:283
  163.1 25.8 %collective-permute-start.46 = (bf16[4,32,2048]{2,1,0:T(8,128)(2,1)}, bf16[4,32,2048]{2,1,0:T(8,128)(2,1)S(1)}, u32[]{:S(2)}, u32[]{:S(2)}) collective-permute-start(bf16[4,32,2048]{2,1,0:T(8,128)(2,1)} %copy-done.38), channel_id=1, source_target_pairs={{0,1},{1,0},{2,3},{3,2},{4,5},{5,4},{6,7},{7,6},{8,9},{9,8},{10,11... | collective-permute-start | bytes 1572872 | tf_op jit(solution)/shard_map/ppermute | solution.py:366
  189.0 7.4 %collective-permute-start.40 = (bf16[32,2048]{1,0:T(8,128)(2,1)S(1)}, bf16[32,2048]{1,0:T(8,128)(2,1)S(1)}, u32[]{:S(2)}, u32[]{:S(2)}) collective-permute-start(bf16[32,2048]{1,0:T(8,128)(2,1)S(1)} %get-tuple-element.213), channel_id=1, source_target_pairs={{0,2},{1,3},{2,0},{3,1},{4,6},{5,7},{6,4},{7,5},{8,10},{9,11},{10,... | collective-permute-start | bytes 393224 | tf_op jit(solution)/shard_map/ppermute | solution.py:342
  189.5 21.0 %collective-permute-start.41 = (bf16[32,2048]{1,0:T(8,128)(2,1)S(1)}, bf16[32,2048]{1,0:T(8,128)(2,1)S(1)}, u32[]{:S(2)}, u32[]{:S(2)}) collective-permute-start(bf16[32,2048]{1,0:T(8,128)(2,1)S(1)} %get-tuple-element.212), channel_id=1, source_target_pairs={{0,4},{1,5},{2,6},{3,7},{4,0},{5,1},{6,2},{7,3},{8,12},{9,13},{10,... | collective-permute-start | bytes 393224 | tf_op jit(solution)/shard_map/ppermute | solution.py:342
  192.1 18.9 %collective-permute-start.42 = (bf16[32,2048]{1,0:T(8,128)(2,1)S(1)}, bf16[32,2048]{1,0:T(8,128)(2,1)S(1)}, u32[]{:S(2)}, u32[]{:S(2)}) collective-permute-start(bf16[32,2048]{1,0:T(8,128)(2,1)S(1)} %get-tuple-element.211), channel_id=1, source_target_pairs={{0,6},{1,7},{2,4},{3,5},{4,2},{5,3},{6,0},{7,1},{8,14},{9,15},{10,... | collective-permute-start | bytes 393224 | tf_op jit(solution)/shard_map/ppermute | solution.py:342
  192.7 18.2 %collective-permute-start.47 = (bf16[32,2048]{1,0:T(8,128)(2,1)S(1)}, bf16[32,2048]{1,0:T(8,128)(2,1)S(1)}, u32[]{:S(2)}, u32[]{:S(2)}) collective-permute-start(bf16[32,2048]{1,0:T(8,128)(2,1)S(1)} %get-tuple-element.216), channel_id=1, source_target_pairs={{0,2},{1,3},{2,0},{3,1},{4,6},{5,7},{6,4},{7,5},{8,10},{9,11},{10,... | collective-permute-start | bytes 393224 | tf_op jit(solution)/shard_map/ppermute | solution.py:342
  194.2 18.6 %collective-permute-start.48 = (bf16[32,2048]{1,0:T(8,128)(2,1)S(1)}, bf16[32,2048]{1,0:T(8,128)(2,1)S(1)}, u32[]{:S(2)}, u32[]{:S(2)}) collective-permute-start(bf16[32,2048]{1,0:T(8,128)(2,1)S(1)} %get-tuple-element.215), channel_id=1, source_target_pairs={{0,4},{1,5},{2,6},{3,7},{4,0},{5,1},{6,2},{7,3},{8,12},{9,13},{10,... | collective-permute-start | bytes 393224 | tf_op jit(solution)/shard_map/ppermute | solution.py:342
  196.4 18.8 %collective-permute-start.49 = (bf16[32,2048]{1,0:T(8,128)(2,1)S(1)}, bf16[32,2048]{1,0:T(8,128)(2,1)S(1)}, u32[]{:S(2)}, u32[]{:S(2)}) collective-permute-start(bf16[32,2048]{1,0:T(8,128)(2,1)S(1)} %get-tuple-element.214), channel_id=1, source_target_pairs={{0,6},{1,7},{2,4},{3,5},{4,2},{5,3},{6,0},{7,1},{8,14},{9,15},{10,... | collective-permute-start | bytes 393224 | tf_op jit(solution)/shard_map/ppermute | solution.py:342
  (59 other events, 303.8 us)
